TPU v7x, 32 devices: a whole 2x2x4 slice. The times are simulated.
32 devices in a mesh: grp: 2 (over y), dev: 16 (over z, x, core).
Axes of the slice: x: 2, y: 2, z: 4, core: 2. Of those that a mesh axis runs over, the one named last changes fastest.
Arguments:
- leaf_right: float32 [32, 8192], P(None, ('grp', 'dev')), may hold values from -6 to 6
- leaf_inverse: float32 [64, 128, 128], P(('grp', 'dev')), may hold values from -1 to 2, as said below
- leaf_link: float32 [64, 128, 128], P(('grp', 'dev')), may hold values from -0.25 to 0.25
- leaf_front: float32 [64, 128, 128], P(('grp', 'dev')), may hold values from -0.375 to 0.375
- parents: int32 [64], P(('grp', 'dev')), may hold values from 1 to 2, as said below
- front_rows: int32 [64], P(('grp', 'dev')), may hold values from 0 to 15
- live_blocks: int32 [32], P(('grp', 'dev')), may hold values from 1 to 2, 56 in all
- front_right: float32 [32, 4096], P(None, ('grp', 'dev')), may hold values from -6 to 6
- front_inverse: float32 [4096, 2048], P(('grp', 'dev')), may hold values from -1 to 2, as said below
- front_couple: float32 [4096, 4096], P(('grp', 'dev')), may hold values from -0.09375 to 0.09375
- root_right: float32 [32, 2, 2048], P(None, None, 'dev'), may hold values from -6 to 6
- root_inverse: float32 [2, 2048, 2048], P(None, 'dev', 'grp'), may hold values from -1 to 2, as said below
- root_couple: float32 [1, 2048, 2048], P(None, 'dev', 'grp'), may hold values from -0.09375 to 0.09375
Outputs:
- leaf_solution: float32 [32, 8192], P(None, ('grp', 'dev'))
- front_solution: float32 [32, 4096], P(None, 'grp')
- root_solution: float32 [32, 2, 2048], P(None, None, 'dev')
Inputs may be any that keep to these rules, and one draw needn't show every extreme that they name: For local block k = b mod 2, parents[b] lies in k + 1 .. 2; the value 2 means no parent among the piece's blocks. A piece's live blocks are its first live_blocks[p]; some piece has all 2. `leaf_inverse`: each block is lower triangular with a positive diagonal. `front_inverse`: each front's block is lower triangular with a positive diagonal. `root_inverse`: each level's block is lower triangular with a positive diagonal.
All inputs are finite; a program needn't handle non-finite values.
Results may differ from a plain program's by a relative error of at most 0.0003.
Values sent between devices are 32-bit elements; how exact they have to be, the bound alone decides.
A program may use at most 64 MiB of HBM per device.

v0:
```python
import jax
import jax.numpy as jnp
from jax import lax
from jax.sharding import PartitionSpec as P

EXACT_ARITHMETIC = lax.Precision.HIGHEST


def front_table(targets, blocks_front):
    return (targets[:, None] == jnp.arange(blocks_front, dtype=jnp.int32)[None, :]).astype(
        jnp.float32
    )


def piece_forward(right_side, inverse, linked, parents, live_count, upper_bound):
    total_blocks = inverse.shape[0]

    def advance(member, loop_state):
        pending, solved = loop_state
        is_alive = member < live_count
        residual = lax.dynamic_index_in_dim(
            right_side, member, 1, False
        ) - lax.dynamic_index_in_dim(pending, member, 1, False)
        solved_block = jnp.where(
            is_alive, jnp.dot(residual, inverse[member], precision=EXACT_ARITHMETIC), 0.0
        )
        solved = lax.dynamic_update_index_in_dim(solved, solved_block, member, 1)
        target = parents[member]
        target_slot = jnp.minimum(target, total_blocks - 1)
        update = jnp.where(
            target < live_count,
            jnp.dot(solved_block, linked[member], precision=EXACT_ARITHMETIC),
            0.0,
        )
        current = lax.dynamic_index_in_dim(pending, target_slot, 1, False)
        pending = lax.dynamic_update_index_in_dim(pending, current + update, target_slot, 1)
        return (pending, solved)

    empty_state = jnp.zeros_like(right_side)
    return lax.fori_loop(0, upper_bound, advance, (empty_state, empty_state))[1]


def piece_backward(base_terms, inverse, linked, parents, live_count, upper_bound):
    total_blocks = inverse.shape[0]

    def retreat(turn_index, solved):
        member = upper_bound - 1 - turn_index
        is_alive = member < live_count
        target = parents[member]
        target_slot = jnp.minimum(target, total_blocks - 1)
        parent_value = lax.dynamic_index_in_dim(solved, target_slot, 1, False)
        carried = jnp.where(
            target < live_count,
            jnp.einsum("rn,mn->rm", parent_value, linked[member], precision=EXACT_ARITHMETIC),
            0.0,
        )
        residual = lax.dynamic_index_in_dim(base_terms, member, 1, False) - carried
        solved_block = jnp.where(
            is_alive,
            jnp.einsum("rn,mn->rm", residual, inverse[member], precision=EXACT_ARITHMETIC),
            0.0,
        )
        return lax.dynamic_update_index_in_dim(solved, solved_block, member, 1)

    return lax.fori_loop(0, upper_bound, retreat, jnp.zeros_like(base_terms))


def front_update(solved, coupled, targets, blocks_front):
    contrib = jnp.einsum("rkn,knm->rkm", solved, coupled, precision=EXACT_ARITHMETIC)
    table = front_table(targets, blocks_front)
    placed = jnp.einsum("rkm,kf->rfm", contrib, table, precision=EXACT_ARITHMETIC)
    return placed.reshape(solved.shape[0], -1)


def front_back(front_values, coupled, targets, blocks_front):
    table = front_table(targets, blocks_front)
    grouped = front_values.reshape(front_values.shape[0], blocks_front, -1)
    picked = jnp.einsum("rfn,kf->rkn", grouped, table, precision=EXACT_ARITHMETIC)
    return jnp.einsum("rkn,kmn->rkm", picked, coupled, precision=EXACT_ARITHMETIC)


def body(
    leaf_right,
    leaf_inverse,
    leaf_link,
    leaf_front,
    parents,
    front_rows,
    live_blocks,
    front_right,
    front_inverse,
    front_couple,
    root_right,
    root_inverse,
    root_couple,
):
    columns = leaf_right.shape[0]
    blocks_here = leaf_inverse.shape[0]
    block_width = leaf_inverse.shape[1]
    front_order = front_inverse.shape[1]
    blocks_front = front_order // block_width
    levels = root_right.shape[1]
    live_count = live_blocks[0]
    right_side = leaf_right.reshape(columns, blocks_here, block_width)
    solved = piece_forward(right_side, leaf_inverse, leaf_link, parents, live_count, live_count)
    partial_front = front_update(solved, leaf_front, front_rows, blocks_front)
    front_share = lax.psum_scatter(partial_front, "dev", scatter_dimension=1, tiled=True)
    front_terms = jnp.dot(front_right - front_share, front_inverse, precision=EXACT_ARITHMETIC)
    forward_front_sweep = lax.psum_scatter(front_terms, "dev", scatter_dimension=1, tiled=True)
    raised_values = jnp.dot(forward_front_sweep, front_couple, precision=EXACT_ARITHMETIC).reshape(
        columns, levels, -1
    )
    pending = lax.psum(
        lax.psum_scatter(raised_values, "dev", scatter_dimension=2, tiled=True), "grp"
    )
    pending_levels = [pending[:, height] for height in range(levels)]
    forward_values = [None] * levels
    for height in reversed(range(levels)):
        residual = root_right[:, height] - pending_levels[height]
        solved_level = lax.psum(
            jnp.dot(residual, root_inverse[height], precision=EXACT_ARITHMETIC), "dev"
        )
        forward_values[height] = solved_level
        if height > 0:
            outgoing = jnp.einsum(
                "rj,mij->rmi", solved_level, root_couple, precision=EXACT_ARITHMETIC
            )
            pushed = lax.psum(outgoing, "grp")
            pending_levels[0] = pending_levels[0] + pushed[:, 0]
    back_values = [None] * levels
    corrections = [jnp.zeros_like(forward_values[0]) for height in range(levels)]
    for height in range(levels):
        residual = forward_values[height] - corrections[height]
        solved_level = lax.psum(
            jnp.einsum("rj,ij->ri", residual, root_inverse[height], precision=EXACT_ARITHMETIC),
            "grp",
        )
        back_values[height] = solved_level
        if height < levels - 1:
            later_levels = list(range(height + 1, levels))
            stacked_blocks = jnp.stack(
                [
                    root_couple[upper_level * (upper_level - 1) // 2 + height]
                    for upper_level in later_levels
                ],
                0,
            )
            outgoing = jnp.einsum(
                "ri,kij->rkj", solved_level, stacked_blocks, precision=EXACT_ARITHMETIC
            )
            pushed = lax.psum(outgoing, "dev")
            for offset, upper_level in enumerate(later_levels):
                corrections[upper_level] = pushed[:, offset]
    root_solution = jnp.stack(back_values, 1)
    grouped_couple = front_couple.reshape(front_couple.shape[0], levels, -1)
    lifted_back = jnp.einsum(
        "rlj,flj->rf",
        lax.all_gather(root_solution, "dev", axis=2, tiled=True),
        grouped_couple,
        precision=EXACT_ARITHMETIC,
    )
    backward_remainder = forward_front_sweep - lifted_back
    front_rows_solved = jnp.einsum(
        "rj,ij->ri",
        lax.all_gather(backward_remainder, "dev", axis=1, tiled=True),
        front_inverse,
        precision=EXACT_ARITHMETIC,
    )
    front_solution = lax.all_gather(front_rows_solved, "dev", axis=1, tiled=True)
    base_terms = solved - front_back(front_solution, leaf_front, front_rows, blocks_front)
    leaf_blocks = piece_backward(
        base_terms, leaf_inverse, leaf_link, parents, live_count, live_count
    )
    return (leaf_blocks.reshape(columns, -1), front_solution, root_solution)


def solution(mesh):
    in_specs = (
        P(None, ("grp", "dev")),
        P(("grp", "dev"), None, None),
        P(("grp", "dev"), None, None),
        P(("grp", "dev"), None, None),
        P(("grp", "dev")),
        P(("grp", "dev")),
        P(("grp", "dev")),
        P(None, ("grp", "dev")),
        P(("grp", "dev"), None),
        P(("grp", "dev"), None),
        P(None, None, "dev"),
        P(None, "dev", "grp"),
        P(None, "dev", "grp"),
    )
    out_specs = (P(None, ("grp", "dev")), P(None, "grp"), P(None, None, "dev"))
    return jax.shard_map(body, mesh=mesh, in_specs=in_specs, out_specs=out_specs, check_vma=False)
```

profile of v0, /device:TPU:1, one launch (start us, length us, event | category | flops | bytes accessed | tf_op | source)
XLA Modules:
  0.0 588.8 jit_solution(9376230081315313895)
XLA Ops:
  8.2 14.0 %while.24 = (s32[]{:T(128)}, f32[32,2,128]{2,0,1:T(8,128)S(1)}, f32[32,2,128]{2,0,1:T(8,128)S(1)}, s32[]{:T(128)}, s32[2]{0:T(128)}, /*index=5*/f32[32,2,128]{2,...) while((s32[]{:T(128)}, f32[32,2,128]{2,0,1:T(8,128)S(1)}, ...), condition=%wide.region_1.2_spmd, body=%wide.region_0.1_spmd.sunk | while | flops 12599307 | bytes 313580 | solution.py:40
  23.7 55.6 %reduce-scatter.4.cloned.1.call-done = f32[32,128]{1,0:T(8,128)} async-done(((f32[32,2048]{1,0:T(8,128)}), f32[32,128]{1,0:T(8,128)}) %reduce-scatter.4.cloned.1.call-update) | async-done | bytes 16400 | tf_op jit(solution)/shard_map/reduce_scatter | solution.py:107
  79.3 2.1 fusion.46
  81.4 56.3 %reduce-scatter.6.cloned.1.call-done = f32[32,128]{1,0:T(8,128)} async-done(((f32[32,2048]{1,0:T(8,128)}), f32[32,128]{1,0:T(8,128)}) %reduce-scatter.6.cloned.1.call-update) | async-done | bytes 16400 | tf_op jit(solution)/shard_map/reduce_scatter | solution.py:109
  137.7 1.9 fusion.55
  140.5 55.6 %reduce-scatter.8.cloned.1.call-done = f32[32,2,128]{2,0,1:T(8,128)} async-done(((f32[32,2,2048]{2,0,1:T(8,128)}), f32[32,2,128]{2,0,1:T(8,128)}) %reduce-scatter.8.cloned.1.call-update) | async-done | bytes 32784 | tf_op jit(solution)/shard_map/reduce_scatter | solution.py:114
  196.1 7.0 %psum.49 = f32[32,2,128]{2,0,1:T(8,128)S(1)} all-reduce(f32[32,2,128]{2,0,1:T(8,128)} %reduce-scatter.8.cloned.1.call-done), channel_id=1, replica_groups=mesh['grp'=2,'dev'=16] {'grp'}, use_global_device_ids=true, to_apply=%region_5.6 | all-reduce | flops 8192 | bytes 65536 | tf_op jit(solution)/shard_map/psum | solution.py:113
  203.1 2.1 fusion.29
  205.3 89.6 %all-reduce.4.cloned.1.call-done = f32[32,1024]{1,0:T(8,128)} async-done(((f32[32,1024]{1,0:T(8,128)}), f32[32,1024]{1,0:T(8,128)}) %all-reduce.4.cloned.1.call-update) | async-done | bytes 131088 | tf_op jit(solution)/shard_map/psum | solution.py:120
  294.9 1.7 convolution_bitcast_fusion.2
  296.6 6.1 %psum.51 = f32[32,1,128]{2,0,1:T(8,128)S(1)} all-reduce(f32[32,1,128]{2,0,1:T(8,128)S(1)} %convolution_bitcast_fusion.2), channel_id=1, replica_groups=mesh['grp'=2,'dev'=16] {'grp'}, use_global_device_ids=true, to_apply=%region_7.8 | all-reduce | flops 4096 | bytes 32768 | tf_op jit(solution)/shard_map/psum | solution.py:128
  302.7 2.1 fusion.23
  304.9 89.8 %all-reduce.6.cloned.1.call-done = f32[32,1024]{1,0:T(8,128)} async-done(((f32[32,1024]{1,0:T(8,128)}), f32[32,1024]{1,0:T(8,128)}) %all-reduce.6.cloned.1.call-update) | async-done | bytes 131088 | tf_op jit(solution)/shard_map/psum | solution.py:120
  396.5 6.1 %psum.53 = f32[32,128]{1,0:T(8,128)S(1)} all-reduce(f32[32,128]{1,0:T(8,128)S(1)} %fusion.21), channel_id=1, replica_groups=mesh['grp'=2,'dev'=16] {'grp'}, use_global_device_ids=true, to_apply=%region_9.10 | all-reduce | flops 4096 | bytes 32768 | tf_op jit(solution)/shard_map/psum | solution.py:134
  402.6 2.1 fusion.25
  404.7 1.9 copy.30
  407.2 87.4 %all-reduce.8.cloned.1.call-done = f32[32,1024]{1,0:T(8,128)} async-done(((f32[32,1024]{1,0:T(8,128)}), f32[32,1024]{1,0:T(8,128)}) %all-reduce.8.cloned.1.call-update) | async-done | bytes 131088 | tf_op jit(solution)/shard_map/psum | solution.py:151
  494.6 1.7 convolution_bitcast_fusion.1
  496.3 6.1 %psum.55 = f32[32,1,128]{2,0,1:T(8,128)S(1)} all-reduce(f32[32,1,128]{2,0,1:T(8,128)S(1)} %convolution_bitcast_fusion.1), channel_id=1, replica_groups=mesh['grp'=2,'dev'=16] {'grp'}, use_global_device_ids=true, to_apply=%region_11.12 | all-reduce | flops 4096 | bytes 32768 | tf_op jit(solution)/shard_map/psum | solution.py:134
  502.4 25.5 %all_gather.9 = f32[32,2,2048]{2,0,1:T(8,128)S(1)} all-gather(f32[32,2,128]{2,0,1:T(8,128)S(1)} %pad_maximum_fusion), channel_id=1, replica_groups=mesh['grp'=2,'dev'=16] {'dev'}, dimensions={2}, use_global_device_ids=true | all-gather | bytes 557056 | tf_op jit(solution)/shard_map/all_gather | solution.py:158
  528.6 2.8 fusion.20
  531.5 18.3 %all_gather.10 = f32[32,2048]{1,0:T(8,128)S(1)} all-gather(f32[32,128]{1,0:T(8,128)S(1)} %fusion.20), channel_id=1, replica_groups=mesh['grp'=2,'dev'=16] {'dev'}, dimensions={1}, use_global_device_ids=true | all-gather | bytes 278528 | tf_op jit(solution)/shard_map/all_gather | solution.py:165
  550.9 19.5 %all_gather.11 = f32[32,2048]{1,0:T(8,128)S(1)} all-gather(f32[32,128]{1,0:T(8,128)S(1)} %fusion.56), channel_id=1, replica_groups=mesh['grp'=2,'dev'=16] {'dev'}, dimensions={1}, use_global_device_ids=true | all-gather | bytes 278528 | tf_op jit(solution)/shard_map/all_gather | solution.py:169
  571.0 9.5 %while.25 = (s32[]{:T(128)}, f32[32,2,128]{2,1,0:T(2,128)S(1)}, s32[]{:T(128)}, s32[]{:T(128)}, f32[32,2,128]{2,0,1:T(8,128)S(1)}, /*index=5*/s32[2]{0:T(128)S(1...) while((s32[]{:T(128)}, f32[32,2,128]{2,1,0:T(2,128)S(1)}, ...), condition=%wide.region_13.14_spmd, body=%wide.region_12.13_spmd.sunk | while | flops 12595212 | bytes 280308 | solution.py:65
  (72 shorter events, 17.8 us)
Async XLA Ops:
  7.2 72.1 %copy-start = (f32[128,2048]{1,0:T(8,128)S(1)}, f32[128,2048]{1,0:T(8,128)}, u32[]{:S(2)}) copy-start(f32[128,2048]{1,0:T(8,128)} %param.25) | copy-start | bytes 3145732
  7.2 15.0 %copy-start.4 = (f32[2,128,128]{2,1,0:T(8,128)S(1)}, f32[2,128,128]{2,1,0:T(8,128)}, u32[]{:S(2)}) copy-start(f32[2,128,128]{2,1,0:T(8,128)} %param.20) | copy-start | bytes 393220
  7.2 15.2 %copy-start.9 = (s32[2]{0:T(128)S(1)}, s32[2]{0:T(128)}, u32[]{:S(2)}) copy-start(s32[2]{0:T(128)} %param.22) | copy-start | bytes 28
  7.2 72.1 %copy-start.8 = (f32[32,128]{1,0:T(8,128)S(1)}, f32[32,128]{1,0:T(8,128)}, u32[]{:S(2)}) copy-start(f32[32,128]{1,0:T(8,128)} %param.24) | copy-start | bytes 49156
  7.2 72.0 %reduce-scatter.4.cloned.1.call-start = ((), (), s32[]{:S(2)}) async-start(), calls=%async_computation.3 | async-start | bytes 278528 | tf_op jit(solution)/shard_map/reduce_scatter | solution.py:107
  8.1 129.5 %copy-start.1 = (f32[128,4096]{1,0:T(8,128)S(1)}, f32[128,4096]{1,0:T(8,128)}, u32[]{:S(2)}) copy-start(f32[128,4096]{1,0:T(8,128)} %param.26) | copy-start | bytes 6291460
  23.6 114.1 %reduce-scatter.6.cloned.1.call-start = ((), (), s32[]{:S(2)}) async-start(), calls=%async_computation.4 | async-start | bytes 278528 | tf_op jit(solution)/shard_map/reduce_scatter | solution.py:109
  81.4 59.1 %copy-start.7 = (f32[32,2,128]{2,1,0:T(2,128)S(1)}, f32[32,2,128]{2,1,0:T(2,128)}, u32[]{:S(2)}) copy-start(f32[32,2,128]{2,1,0:T(2,128)} %param.27) | copy-start | bytes 98308
  81.4 114.8 %reduce-scatter.8.cloned.1.call-start = ((), (), s32[]{:S(2)}) async-start(), calls=%async_computation.5 | async-start | bytes 557056 | tf_op jit(solution)/shard_map/reduce_scatter | solution.py:114
  140.4 154.4 %all-reduce.4.cloned.1.call-start = ((), (), s32[]{:S(2)}) async-start(), calls=%async_computation.6 | async-start | bytes 262144 | tf_op jit(solution)/shard_map/psum | solution.py:120
  205.2 189.5 %all-reduce.6.cloned.1.call-start = ((), (), s32[]{:S(2)}) async-start(), calls=%async_computation.7 | async-start | bytes 262144 | tf_op jit(solution)/shard_map/psum | solution.py:120
  304.8 189.7 %all-reduce.8.cloned.1.call-start = ((), (), s32[]{:S(2)}) async-start(), calls=%async_computation.8 | async-start | bytes 262144 | tf_op jit(solution)/shard_map/psum | solution.py:151
  404.7 89.9 %copy-start.5 = (f32[32,1024]{1,0:T(8,128)S(1)}, f32[32,1024]{1,0:T(8,128)}, u32[]{:S(2)}) copy-start(f32[32,1024]{1,0:T(8,128)} %all-reduce.4.cloned.1.call-done) | copy-start | bytes 393220
  404.7 123.9 %copy-start.6 = (f32[32,128]{1,0:T(8,128)S(1)}, f32[32,128]{1,0:T(8,128)}, u32[]{:S(2)}) copy-start(f32[32,128]{1,0:T(8,128)} %reduce-scatter.6.cloned.1.call-done) | copy-start | bytes 49156
  531.4 39.6 %copy-start.2 = (f32[2,128,128]{2,1,0:T(8,128)S(1)}, f32[2,128,128]{2,1,0:T(8,128)}, u32[]{:S(2)}) copy-start(f32[2,128,128]{2,1,0:T(8,128)} %get-tuple-element.371) | copy-start | bytes 393220
  531.4 39.6 %copy-start.3 = (f32[2,128,128]{2,1,0:T(8,128)S(1)}, f32[2,128,128]{2,1,0:T(8,128)}, u32[]{:S(2)}) copy-start(f32[2,128,128]{2,1,0:T(8,128)} %get-tuple-element.372) | copy-start | bytes 393220
  531.5 39.6 %copy-start.10 = (s32[2]{0:T(128)S(1)}, s32[2]{0:T(128)}, u32[]{:S(2)}) copy-start(s32[2]{0:T(128)} %get-tuple-element.391) | copy-start | bytes 28
Sparse Core Ops, SparseCore 0:
  23.8 55.4 reduce-scatter.3
  83.3 54.3 reduce-scatter.5
  141.2 54.8 reduce-scatter.7
  205.3 89.4 all-reduce.3
  305.0 89.7 all-reduce.5
  404.8 89.7 all-reduce.7
where the time goes:
time: 590 us; the launch traced here: 589 us
  waiting for transfers between devices  434 us (74%)
  blocking collectives  88.6 us (15%)
  matrix products  25.4 us (4%)
  between operations  15 us (3%)
  loops' own time  14.7 us (2%)
  local copies, waits for them, and re-layouts  10.4 us (2%)
    psum x2, waiting for transfers between devices, body(): lax.psum(jnp.dot(residual, root_inverse[height], precision=EXACT_ARITHMET...  179 us
    psum x1, waiting for transfers between devices, body(): pushed = lax.psum(outgoing, 'dev')  87.4 us
    reduce_scatter x1, waiting for transfers between devices, body(): lax.psum_scatter(front_terms, 'dev', scatter_dimension=1, tiled=True)  56.3 us
    reduce_scatter x1, waiting for transfers between devices, body(): lax.psum_scatter(raised_values, 'dev', scatter_dimension=2, tiled=True)  55.6 us
    reduce_scatter x1, waiting for transfers between devices, body(): lax.psum_scatter(partial_front, 'dev', scatter_dimension=1, tiled=True)  55.6 us
    all_gather x1, blocking collectives, body(): lax.all_gather(root_solution, 'dev', axis=2, tiled=True)  25.5 us
    all_gather x1, blocking collectives, body(): lax.all_gather(front_rows_solved, 'dev', axis=1, tiled=True)  19.5 us
    all_gather x1, blocking collectives, body(): lax.all_gather(backward_remainder, 'dev', axis=1, tiled=True)  18.3 us
  transfers between devices with their start and end apart: 6, of which 6 were waited for; matrix products, arithmetic and copies ran while one was open for 0% of the time, Pallas kernels for 0%

commit v1 on v0

v1 whole, which is shorter than its diff:
```python
import functools

import jax
import jax.numpy as jnp
from jax import lax
from jax.experimental import pallas as pl
from jax.experimental.pallas import tpu as pltpu
from jax.sharding import PartitionSpec as P

MESH = pl.DeviceIdType.MESH
ROW_TILE = 8
F32 = jnp.float32
BF16 = jnp.bfloat16

(
    FRONT_SUM,
    FRONT_SOLVE,
    RAISE_TOP,
    RAISE_LOW,
    RAISE_TOP_GRP,
    RAISE_LOW_GRP,
    TOP_SUM,
    TOP_SHARE,
    PUSH_GRP,
    LOW_SUM,
    LOW_SHARE,
    LOW_BACK_GRP,
    CORRECT_SUM,
    CORRECT_SHARE,
    LOW_ALL,
    TOP_BACK_GRP,
    TOP_ALL,
    REMAINDER_ALL,
    FRONT_ALL,
    PHASES,
) = range(20)


def split(values):
    high = values.astype(BF16)
    return high, (values - high.astype(F32)).astype(BF16)


def product(left, high, low, transposed=False):
    rows = left.shape[0]
    left_high, left_low = split(left)
    contract = (((1,), (1 if transposed else 0,)), ((), ()))
    both = lax.dot_general(
        jnp.concatenate([left_high, left_low], 0), high, contract, preferred_element_type=F32
    )
    rest = lax.dot_general(left_high, low, contract, preferred_element_type=F32)
    return both[:rows] + both[rows:] + rest


def kernel(
    groups,
    devs,
    parents,
    targets,
    live_blocks,
    root_right,
    leaf_right_hbm,
    leaf_inverse_hbm,
    leaf_link_hbm,
    leaf_front_hbm,
    front_right_hbm,
    front_inverse_hbm,
    front_couple_hbm,
    root_inverse_hbm,
    root_couple_hbm,
    leaf_out,
    front_out,
    root_out,
    leaf_right,
    leaf_inverse,
    leaf_link,
    leaf_front,
    front_right,
    front_inverse,
    front_couple,
    root_inverse,
    root_couple,
    fi_high,
    fi_low,
    fc_high,
    fc_low,
    ri_high,
    ri_low,
    rc_high,
    rc_low,
    solved,
    front_sum_part,
    front_sum_got,
    front_solve_part,
    front_solve_got,
    raise_top_part,
    raise_top_got,
    raise_low_part,
    raise_low_got,
    top_part,
    top_got,
    top_share,
    low_part,
    low_got,
    low_share,
    correct_part,
    correct_got,
    correct_share,
    raise_top_grp,
    raise_low_grp,
    push_grp,
    low_back_grp,
    top_back_grp,
    low_all,
    top_all,
    remainder_all,
    front_all,
    load_sem,
    send_sem,
    recv_sem,
):
    group = lax.axis_index("grp")
    me = lax.axis_index("dev")
    columns = leaf_right.shape[0]
    blocks_here, width = leaf_inverse.shape[0], leaf_inverse.shape[1]
    front_order = front_inverse.shape[1]
    blocks_front = front_order // width
    front_part = front_right.shape[1]
    level_rows = front_couple.shape[1] // 2
    level_part = level_rows // devs
    level_columns = root_inverse.shape[2]
    row_tiles = columns // ROW_TILE
    piece = top_part.shape[2]

    loads = [
        pltpu.make_async_copy(source, target, load_sem.at[place])
        for place, (source, target) in enumerate(
            (
                (leaf_right_hbm, leaf_right),
                (leaf_inverse_hbm, leaf_inverse),
                (leaf_link_hbm, leaf_link),
                (leaf_front_hbm, leaf_front),
                (front_right_hbm, front_right),
                (front_inverse_hbm, front_inverse),
                (front_couple_hbm, front_couple),
                (root_inverse_hbm, root_inverse),
                (root_couple_hbm, root_couple),
            )
        )
    ]
    for load in loads:
        load.start()

    barrier = pltpu.get_barrier_semaphore()

    def greet_dev(step, carry):
        pl.semaphore_signal(
            barrier, inc=1, device_id=(group, lax.rem(me + step, devs)), device_id_type=MESH
        )
        return carry

    def greet_grp(step, carry):
        pl.semaphore_signal(
            barrier, inc=1, device_id=(lax.rem(group + step, groups), me), device_id_type=MESH
        )
        return carry

    lax.fori_loop(1, devs, greet_dev, 0)
    lax.fori_loop(1, groups, greet_grp, 0)

    def scatter(phase, part, got):
        def one(step, carry):
            peer = lax.rem(me + step, devs)
            pltpu.make_async_remote_copy(
                src_ref=part.at[peer],
                dst_ref=got.at[step],
                send_sem=send_sem.at[phase],
                recv_sem=recv_sem.at[phase],
                device_id=(group, peer),
                device_id_type=MESH,
            ).start()
            return carry

        lax.fori_loop(1, devs, one, 0)
        got[0] = part[me]

    def share(phase, values, buffer):
        buffer[me] = values

        def one(step, carry):
            pltpu.make_async_remote_copy(
                src_ref=buffer.at[me],
                dst_ref=buffer.at[me],
                send_sem=send_sem.at[phase],
                recv_sem=recv_sem.at[phase],
                device_id=(group, lax.rem(me + step, devs)),
                device_id_type=MESH,
            ).start()
            return carry

        lax.fori_loop(1, devs, one, 0)

    def share_grp(phase, values, buffer):
        buffer[group] = values

        def one(step, carry):
            pltpu.make_async_remote_copy(
                src_ref=buffer.at[group],
                dst_ref=buffer.at[group],
                send_sem=send_sem.at[phase],
                recv_sem=recv_sem.at[phase],
                device_id=(lax.rem(group + step, groups), me),
                device_id_type=MESH,
            ).start()
            return carry

        lax.fori_loop(1, groups, one, 0)

    def settle(semaphore, phase, buffer):
        some = buffer.at[pl.ds(1, buffer.shape[0] - 1)]
        pltpu.make_async_copy(some, some, semaphore.at[phase]).wait()

    def total(phase, buffer):
        settle(recv_sem, phase, buffer)
        result = buffer[0]
        for place in range(1, buffer.shape[0]):
            result = result + buffer[place]
        return result

    def arrived(phase, buffer):
        settle(recv_sem, phase, buffer)
        return jnp.concatenate([buffer[place] for place in range(buffer.shape[0])], 1)

    def split_rows(source, high, low):
        step_rows = 2 * ROW_TILE

        def one(step, carry):
            rows = pl.ds(pl.multiple_of(step * step_rows, step_rows), step_rows)
            high[rows, :], low[rows, :] = split(source[rows, :])
            return carry

        lax.fori_loop(0, source.shape[0] // step_rows, one, 0)

    def spread(left, high, low, start, part, span):
        count = part.shape[0] * span
        chunk = min(count, 512)
        for at in range(0, count, chunk):
            here = product(
                left, high[:, start + at : start + at + chunk], low[:, start + at : start + at + chunk]
            )
            for block in range(chunk // span):
                part[at // span + block] = here[:, block * span : (block + 1) * span]

    def spread_pieces(left, high, low, part):
        here = product(left, high[...], low[...])
        for across in range(devs // row_tiles):
            for down in range(row_tiles):
                part[across * row_tiles + down] = here[
                    down * ROW_TILE : (down + 1) * ROW_TILE, across * piece : (across + 1) * piece
                ]

    def arrived_pieces(phase, buffer):
        settle(recv_sem, phase, buffer)
        return jnp.concatenate(
            [
                jnp.concatenate(
                    [buffer[across * row_tiles + down] for down in range(row_tiles)], 0
                )
                for across in range(devs // row_tiles)
            ],
            1,
        )

    live = live_blocks[0]
    for place in range(4):
        loads[place].wait()
    updates = []
    contributions = []
    for k in range(blocks_here):
        residual = leaf_right[:, k * width : (k + 1) * width]
        for child in range(k):
            residual = residual - jnp.where(parents[child] == k, updates[child], 0.0)
        block = jnp.where(k < live, product(residual, *split(leaf_inverse[k])), 0.0)
        solved[k] = block
        if k < blocks_here - 1:
            updates.append(product(block, *split(leaf_link[k])))
        contributions.append(product(block, *split(leaf_front[k])))
    spans = width // front_part
    for block in range(blocks_front):
        placed = jnp.zeros((columns, width), F32)
        for k in range(blocks_here):
            placed = placed + jnp.where(targets[k] == block, contributions[k], 0.0)
        for within in range(spans):
            front_sum_part[block * spans + within] = placed[
                :, within * front_part : (within + 1) * front_part
            ]

    pl.semaphore_wait(barrier, devs - 1 + groups - 1)
    scatter(FRONT_SUM, front_sum_part, front_sum_got)

    loads[4].wait()
    loads[5].wait()
    split_rows(front_inverse, fi_high, fi_low)
    residual = front_right[...] - total(FRONT_SUM, front_sum_got)
    spread(residual, fi_high, fi_low, 0, front_solve_part, front_part)
    scatter(FRONT_SOLVE, front_solve_part, front_solve_got)
    loads[6].wait()
    split_rows(front_couple, fc_high, fc_low)
    front_forward = total(FRONT_SOLVE, front_solve_got)

    spread(front_forward, fc_high, fc_low, level_rows, raise_top_part, level_part)
    scatter(RAISE_TOP, raise_top_part, raise_top_got)
    spread(front_forward, fc_high, fc_low, 0, raise_low_part, level_part)
    loads[7].wait()
    loads[8].wait()
    for level in range(2):
        split_rows(root_inverse.at[level], ri_high.at[level], ri_low.at[level])
    split_rows(root_couple.at[0], rc_high, rc_low)
    raised_top = total(RAISE_TOP, raise_top_got)
    share_grp(RAISE_TOP_GRP, raised_top, raise_top_grp)
    scatter(RAISE_LOW, raise_low_part, raise_low_got)

    residual = root_right[:, 1, :] - total(RAISE_TOP_GRP, raise_top_grp)
    spread_pieces(residual, ri_high[1], ri_low[1], top_part)
    scatter(TOP_SUM, top_part, top_got)
    share_grp(RAISE_LOW_GRP, total(RAISE_LOW, raise_low_got), raise_low_grp)
    share(TOP_SHARE, total(TOP_SUM, top_got), top_share)
    low_right = root_right[:, 0, :] - total(RAISE_LOW_GRP, raise_low_grp)
    top_forward = arrived_pieces(TOP_SHARE, top_share)

    share_grp(PUSH_GRP, product(top_forward, rc_high[...], rc_low[...], True), push_grp)
    residual = low_right - total(PUSH_GRP, push_grp)
    spread_pieces(residual, ri_high[0], ri_low[0], low_part)
    scatter(LOW_SUM, low_part, low_got)
    share(LOW_SHARE, total(LOW_SUM, low_got), low_share)
    low_forward = arrived_pieces(LOW_SHARE, low_share)

    share_grp(LOW_BACK_GRP, product(low_forward, ri_high[0], ri_low[0], True), low_back_grp)
    low_solution = total(LOW_BACK_GRP, low_back_grp)
    root_out[:, 0, :] = low_solution
    spread_pieces(low_solution, rc_high[...], rc_low[...], correct_part)
    scatter(CORRECT_SUM, correct_part, correct_got)
    share(LOW_ALL, low_solution, low_all)
    share(CORRECT_SHARE, total(CORRECT_SUM, correct_got), correct_share)
    lifted = product(
        arrived(LOW_ALL, low_all), fc_high[:, :level_rows], fc_low[:, :level_rows], True
    )
    residual = top_forward - arrived_pieces(CORRECT_SHARE, correct_share)
    share_grp(TOP_BACK_GRP, product(residual, ri_high[1], ri_low[1], True), top_back_grp)
    top_solution = total(TOP_BACK_GRP, top_back_grp)
    share(TOP_ALL, top_solution, top_all)
    root_out[:, 1, :] = top_solution

    lifted = lifted + product(
        arrived(TOP_ALL, top_all), fc_high[:, level_rows:], fc_low[:, level_rows:], True
    )
    share(REMAINDER_ALL, front_forward - lifted, remainder_all)
    remainder = arrived(REMAINDER_ALL, remainder_all)
    share(FRONT_ALL, product(remainder, fi_high[...], fi_low[...], True), front_all)
    front_out[...] = arrived(FRONT_ALL, front_all)

    solutions = [None] * blocks_here
    for k in reversed(range(blocks_here)):
        picked = jnp.zeros((columns, width), F32)
        for block in range(blocks_front):
            picked = picked + jnp.where(
                targets[k] == block, front_out[:, block * width : (block + 1) * width], 0.0
            )
        residual = solved[k] - product(picked, *split(leaf_front[k]), True)
        if k < blocks_here - 1:
            above = jnp.zeros((columns, width), F32)
            for other in range(k + 1, blocks_here):
                above = above + jnp.where(parents[k] == other, solutions[other], 0.0)
            residual = residual - product(above, *split(leaf_link[k]), True)
        solutions[k] = jnp.where(k < live, product(residual, *split(leaf_inverse[k]), True), 0.0)
        leaf_out[:, k * width : (k + 1) * width] = solutions[k]

    for phase, buffer in (
        (FRONT_SUM, front_sum_part),
        (FRONT_SOLVE, front_solve_part),
        (RAISE_TOP, raise_top_part),
        (RAISE_LOW, raise_low_part),
        (RAISE_TOP_GRP, raise_top_grp),
        (RAISE_LOW_GRP, raise_low_grp),
        (TOP_SUM, top_part),
        (TOP_SHARE, top_share),
        (PUSH_GRP, push_grp),
        (LOW_SUM, low_part),
        (LOW_SHARE, low_share),
        (LOW_BACK_GRP, low_back_grp),
        (CORRECT_SUM, correct_part),
        (CORRECT_SHARE, correct_share),
        (LOW_ALL, low_all),
        (TOP_BACK_GRP, top_back_grp),
        (TOP_ALL, top_all),
        (REMAINDER_ALL, remainder_all),
        (FRONT_ALL, front_all),
    ):
        settle(send_sem, phase, buffer)


def body(
    groups,
    devs,
    leaf_right,
    leaf_inverse,
    leaf_link,
    leaf_front,
    parents,
    front_rows,
    live_blocks,
    front_right,
    front_inverse,
    front_couple,
    root_right,
    root_inverse,
    root_couple,
):
    columns = leaf_right.shape[0]
    front_part = front_right.shape[1]
    level_part = root_right.shape[2]
    level_columns = root_inverse.shape[2]
    row_tiles = columns // ROW_TILE
    piece = level_columns * row_tiles // devs
    loaded = (
        leaf_right,
        leaf_inverse,
        leaf_link,
        leaf_front,
        front_right,
        front_inverse,
        front_couple,
        root_inverse,
        root_couple,
    )
    in_halves = (front_inverse, front_couple, root_inverse, root_couple[0])
    front_blocks = pltpu.VMEM((devs, columns, front_part), F32)
    level_blocks = pltpu.VMEM((devs, columns, level_part), F32)
    pieces = pltpu.VMEM((devs, ROW_TILE, piece), F32)
    grp_blocks = pltpu.VMEM((groups, columns, level_part), F32)
    vmem = pl.BlockSpec(memory_space=pltpu.VMEM)
    smem = pl.BlockSpec(memory_space=pltpu.SMEM)
    anywhere = pl.BlockSpec(memory_space=pl.ANY)
    return pl.pallas_call(
        functools.partial(kernel, groups, devs),
        out_shape=(
            jax.ShapeDtypeStruct(leaf_right.shape, F32),
            jax.ShapeDtypeStruct((columns, front_part * devs), F32),
            jax.ShapeDtypeStruct(root_right.shape, F32),
        ),
        in_specs=[smem] * 3 + [vmem] + [anywhere] * len(loaded),
        out_specs=(vmem, vmem, vmem),
        scratch_shapes=[pltpu.VMEM(array.shape, F32) for array in loaded]
        + [pltpu.VMEM(array.shape, BF16) for array in in_halves for _ in range(2)]
        + [pltpu.VMEM((leaf_inverse.shape[0], columns, leaf_inverse.shape[1]), F32)]
        + [front_blocks] * 4
        + [level_blocks] * 4
        + [pieces] * 9
        + [grp_blocks] * 5
        + [level_blocks] * 2
        + [front_blocks] * 2
        + [
            pltpu.SemaphoreType.DMA((len(loaded),)),
            pltpu.SemaphoreType.DMA((PHASES,)),
            pltpu.SemaphoreType.DMA((PHASES,)),
        ],
        compiler_params=pltpu.CompilerParams(
            collective_id=0, has_side_effects=True, vmem_limit_bytes=48 * 1024 * 1024
        ),
        name="block_solves",
    )(parents, front_rows, live_blocks, root_right, *loaded)


def solution(mesh):
    in_specs = (
        P(None, ("grp", "dev")),
        P(("grp", "dev"), None, None),
        P(("grp", "dev"), None, None),
        P(("grp", "dev"), None, None),
        P(("grp", "dev")),
        P(("grp", "dev")),
        P(("grp", "dev")),
        P(None, ("grp", "dev")),
        P(("grp", "dev"), None),
        P(("grp", "dev"), None),
        P(None, None, "dev"),
        P(None, "dev", "grp"),
        P(None, "dev", "grp"),
    )
    out_specs = (P(None, ("grp", "dev")), P(None, "grp"), P(None, None, "dev"))
    return jax.shard_map(
        functools.partial(body, mesh.shape["grp"], mesh.shape["dev"]),
        mesh=mesh,
        in_specs=in_specs,
        out_specs=out_specs,
        check_vma=False,
    )
```

time: 590 us -> 115 us (0.19)
  waiting for transfers between devices: 434 us -> 0 us
  Pallas kernels: 0 us -> 99.3 us
  blocking collectives: 88.6 us -> 0 us
  matrix products: 25.4 us -> 0 us
  loops' own time: 14.7 us -> 0 us
  between operations: 15 us -> 1.31 us
    psum x3 -> x0, waiting for transfers between devices: 267 us -> none  [the longest x2 179 us: body(): lax.psum(jnp.dot(residual, root_inverse[height], precision=EXACT_ARITHMET...]
    reduce_scatter x3 -> x0, waiting for transfers between devices: 167 us -> none  [the longest x1 56.3 us: body(): lax.psum_scatter(front_terms, 'dev', scatter_dimension=1, tiled=True)]
    pallas_call x0 -> x1, Pallas kernels: none -> 99.3 us  [body(): pl.pallas_call(functools.partial(kernel, groups, devs), out_shape=(jax.Sh...]
    all_gather x3 -> x0, blocking collectives: 63.3 us -> none  [the longest x1 25.5 us: body(): lax.all_gather(root_solution, 'dev', axis=2, tiled=True)]
    dot_general x22 -> x0, matrix products: 25.4 us -> none  [the longest x2 4.19 us: body(): jnp.dot(residual, root_inverse[height], precision=EXACT_ARITHMETIC)]
    psum x4 -> x0, blocking collectives: 25.3 us -> none  [the longest x2 12.2 us: body(): lax.psum(jnp.einsum('rj,ij->ri', residual, root_inverse[height], precisio...]
    another operation x2 -> x0, loops' own time: 14.7 us -> none  [the longest x1 7.4 us: piece_forward(): return lax.fori_loop(0, upper_bound, advance, (empty_state, empty_state))[1]]
    unnamed x27, local copies, waits for them, and re-layouts: 2.86 us -> 13.3 us
  transfers between devices with their start and end apart: 6 -> 0, of which waited for: 6 -> 0; matrix products, arithmetic and copies ran while one was open for 0% -> 0% of each run, Pallas kernels for 0% -> 0%
where the time goes in v1:
time: 115 us; the launch traced here: 114 us
  Pallas kernels  99.3 us (86%)
  local copies, waits for them, and re-layouts  13.3 us (12%)
  between operations  1.31 us (1%)
    pallas_call x1, Pallas kernels, body(): pl.pallas_call(functools.partial(kernel, groups, devs), out_shape=(jax.Sh...  99.3 us
    unnamed x27, local copies, waits for them, and re-layouts  13.3 us

profile of v1, /device:TPU:1, one launch (start us, length us, event | category | flops | bytes accessed | tf_op | source)
XLA Modules:
  0.0 113.9 jit_solution(1415748539557630922)
XLA Ops:
  1.3 0.0 copy-start
  1.3 1.6 %copy-done = f32[128,4096]{1,0:T(8,128)S(1)} copy-done((f32[128,4096]{1,0:T(8,128)S(1)}, f32[128,4096]{1,0:T(8,128)}, u32[]{:S(2)}) %copy-start) | copy-done | bytes 2097176
  2.9 0.0 copy-start.1
  2.9 1.2 %copy-done.1 = f32[128,2048]{1,0:T(8,128)S(1)} copy-done((f32[128,2048]{1,0:T(8,128)S(1)}, f32[128,2048]{1,0:T(8,128)}, u32[]{:S(2)}) %copy-start.1) | copy-done | bytes 1048600
  4.1 0.0 copy-start.2
  4.1 1.2 %copy-done.2 = f32[2,128,1024]{2,1,0:T(8,128)S(1)} copy-done((f32[2,128,1024]{2,1,0:T(8,128)S(1)}, f32[2,128,1024]{2,1,0:T(8,128)}, u32[]{:S(2)}) %copy-start.2) | copy-done | bytes 1048600
  5.3 0.0 copy-start.3
  5.3 1.0 copy-done.3
  6.4 0.0 copy-start.4
  6.4 0.9 copy-done.4
  7.3 0.0 copy-start.5
  7.3 0.9 copy-done.5
  8.2 0.0 copy-start.6
  8.2 0.9 copy-done.6
  9.1 0.0 copy-start.7
  9.1 0.8 copy-done.7
  9.8 0.8 copy-done.8
  10.6 0.7 copy-done.9
  11.3 0.7 copy-done.10
  12.0 0.7 copy-done.11
  12.6 99.3 %block_solves.1 = (f32[32,256]{1,0:T(8,128)S(1)}, f32[32,2048]{1,0:T(8,128)S(1)}, f32[32,2,128]{2,1,0:T(2,128)S(1)}) custom-call(s32[2]{0:T(128)S(1)} %copy-done.10, s32[2]{0:T(128)S(1)} %copy-done.11, s32[1]{0:T(128)S(6)} %copy.19.live_blocks, f32[32,2,128]{2,1,0:T(2,128)S(1)} %copy-done.7, f32[32,256]{1,0:T(8,128)S(1)} %copy-done.8, ...), custom_call_target="tpu_custom_call" | custom-call | tf_op jit(solution)/shard_map/block_solves/pallas_call | solution.py:444
  112.0 0.6 copy.20
  112.6 0.7 copy.21
  113.3 0.6 copy.22
  (4 shorter events, 0.0 us)
Async XLA Ops:
  1.3 1.6 %copy-start = (f32[128,4096]{1,0:T(8,128)S(1)}, f32[128,4096]{1,0:T(8,128)}, u32[]{:S(2)}) copy-start(f32[128,4096]{1,0:T(8,128)} %front_couple_hbm.1) | copy-start | bytes 6291460
  2.9 1.2 %copy-start.1 = (f32[128,2048]{1,0:T(8,128)S(1)}, f32[128,2048]{1,0:T(8,128)}, u32[]{:S(2)}) copy-start(f32[128,2048]{1,0:T(8,128)} %front_inverse_hbm.1) | copy-start | bytes 3145732
  4.1 1.2 %copy-start.2 = (f32[2,128,1024]{2,1,0:T(8,128)S(1)}, f32[2,128,1024]{2,1,0:T(8,128)}, u32[]{:S(2)}) copy-start(f32[2,128,1024]{2,1,0:T(8,128)} %root_inverse_hbm.1) | copy-start | bytes 3145732
  5.3 1.0 copy-start.3
  6.4 0.9 copy-start.4
  7.3 0.9 copy-start.5
  8.2 0.9 copy-start.6
  9.1 0.8 copy-start.7
  9.8 0.8 copy-start.8
  10.6 0.7 copy-start.9
  11.3 0.7 copy-start.10
  12.0 0.7 copy-start.11

commit v2 on v1

v2 whole, which is shorter than its diff:
```python
import functools

import jax
import jax.numpy as jnp
from jax import lax
from jax.experimental import pallas as pl
from jax.experimental.pallas import tpu as pltpu
from jax.sharding import PartitionSpec as P

MESH = pl.DeviceIdType.MESH
ROW_TILE = 8
F32 = jnp.float32
BF16 = jnp.bfloat16

(
    FRONT_SUM,
    FRONT_SOLVE,
    RAISE_TOP,
    RAISE_LOW,
    RAISE_TOP_GRP,
    RAISE_LOW_GRP,
    TOP_SUM,
    TOP_SHARE,
    PUSH_GRP,
    LOW_SUM,
    LOW_SHARE,
    LOW_BACK_GRP,
    CORRECT_SUM,
    CORRECT_SHARE,
    LOW_ALL,
    TOP_BACK_GRP,
    TOP_ALL,
    REMAINDER_ALL,
    FRONT_ALL,
    PHASES,
) = range(20)


def split(values):
    high = values.astype(BF16)
    return high, (values - high.astype(F32)).astype(BF16)


def product(left, high, low, transposed=False):
    rows = left.shape[0]
    left_high, left_low = split(left)
    contract = (((1,), (1 if transposed else 0,)), ((), ()))
    both = lax.dot_general(
        jnp.concatenate([left_high, left_low], 0), high, contract, preferred_element_type=F32
    )
    rest = lax.dot_general(left_high, low, contract, preferred_element_type=F32)
    return both[:rows] + both[rows:] + rest


def kernel(
    groups,
    devs,
    parents,
    targets,
    live_blocks,
    root_right,
    leaf_right_hbm,
    leaf_inverse_hbm,
    leaf_link_hbm,
    leaf_front_hbm,
    front_right_hbm,
    front_inverse_hbm,
    front_couple_hbm,
    root_inverse_hbm,
    root_couple_hbm,
    leaf_out,
    front_out,
    root_out,
    leaf_right,
    leaf_inverse,
    leaf_link,
    leaf_front,
    front_right,
    front_inverse,
    front_couple,
    root_inverse,
    root_couple,
    fi_high,
    fi_low,
    fc_high,
    fc_low,
    ri_high,
    ri_low,
    rc_high,
    rc_low,
    solved,
    front_sum_part,
    front_solve_part,
    front_sum_pair,
    front_sum_got,
    front_solve_pair,
    front_solve_got,
    raise_top_part,
    raise_low_part,
    raise_top_pair,
    raise_top_got,
    raise_low_pair,
    raise_low_got,
    top_part,
    low_part,
    correct_part,
    top_share,
    low_share,
    correct_share,
    top_pair,
    top_got,
    low_pair,
    low_got,
    correct_pair,
    correct_got,
    raise_top_grp,
    raise_low_grp,
    push_grp,
    low_back_grp,
    top_back_grp,
    low_all,
    top_all,
    remainder_all,
    front_all,
    load_sem,
    send_sem,
    recv_sem,
    pair_send_sem,
    pair_recv_sem,
):
    group = lax.axis_index("grp")
    me = lax.axis_index("dev")
    chips = devs // 2
    chip = me // 2
    core = lax.rem(me, 2)
    other = 1 - core
    sibling = (group, chip * 2 + other)
    columns = leaf_right.shape[0]
    blocks_here, width = leaf_inverse.shape[0], leaf_inverse.shape[1]
    blocks_front = front_inverse.shape[1] // width
    front_part = front_right.shape[1]
    level_rows = front_couple.shape[1] // 2
    row_tiles = columns // ROW_TILE
    piece = top_part.shape[3]

    def chip_peer(step):
        return (group, lax.rem(chip + step, chips) * 2 + core)

    def grp_peer(step):
        return (lax.rem(group + step, groups), me)

    loads = [
        pltpu.make_async_copy(source, target, load_sem.at[place])
        for place, (source, target) in enumerate(
            (
                (leaf_right_hbm, leaf_right),
                (leaf_inverse_hbm, leaf_inverse),
                (leaf_link_hbm, leaf_link),
                (leaf_front_hbm, leaf_front),
                (front_right_hbm, front_right),
                (front_inverse_hbm, front_inverse),
                (front_couple_hbm, front_couple),
                (root_inverse_hbm, root_inverse),
                (root_couple_hbm, root_couple),
            )
        )
    ]
    for load in loads:
        load.start()

    barrier = pltpu.get_barrier_semaphore()

    def greet(device):
        pl.semaphore_signal(barrier, inc=1, device_id=device, device_id_type=MESH)

    greet(sibling)
    for step in range(1, chips):
        greet(chip_peer(step))
    for step in range(1, groups):
        greet(grp_peer(step))

    def send(source, target, device, phase):
        pltpu.make_async_remote_copy(
            src_ref=source,
            dst_ref=target,
            send_sem=send_sem.at[phase],
            recv_sem=recv_sem.at[phase],
            device_id=device,
            device_id_type=MESH,
        ).start()

    def send_pair(source, target, phase):
        pltpu.make_async_remote_copy(
            src_ref=source,
            dst_ref=target,
            send_sem=pair_send_sem.at[phase],
            recv_sem=pair_recv_sem.at[phase],
            device_id=sibling,
            device_id_type=MESH,
        ).start()

    def settle(semaphore, some):
        pltpu.make_async_copy(some, some, semaphore).wait()

    def pair_sum(phase, part, pair, fill):
        fill(other, part.at[other])
        send_pair(part.at[other], pair, phase)
        fill(core, part.at[core])

    def chip_send(phase, part, got):
        for step in range(1, chips):
            peer = lax.rem(chip + step, chips)
            send(part.at[core, peer], got.at[step], chip_peer(step), phase)

    def pair_done(phase, part, pair):
        settle(pair_recv_sem.at[phase], pair)
        for place in range(chips):
            part[core, place] = part[core, place] + pair[place]

    def total(phase, part, got):
        result = part[core, chip]
        settle(recv_sem.at[phase], got.at[pl.ds(1, chips - 1)])
        for place in range(1, chips):
            result = result + got[place]
        return result

    def share(phase, values, buffer):
        buffer[core, chip] = values
        for step in range(1, chips):
            send(buffer.at[core, chip], buffer.at[core, chip], chip_peer(step), phase)

    def share_pair(phase, buffer):
        settle(recv_sem.at[phase], buffer.at[0, pl.ds(1, chips - 1)])
        send_pair(buffer.at[core], buffer.at[core], phase)

    def pair_arrived(phase, buffer):
        settle(pair_recv_sem.at[phase], buffer.at[0])

    def share_grp(phase, values, buffer):
        buffer[group] = values
        for step in range(1, groups):
            send(buffer.at[group], buffer.at[group], grp_peer(step), phase)

    def total_grp(phase, buffer):
        settle(recv_sem.at[phase], buffer.at[pl.ds(1, groups - 1)])
        result = buffer[0]
        for place in range(1, groups):
            result = result + buffer[place]
        return result

    def whole(buffer, half):
        return jnp.concatenate([buffer[half, place] for place in range(chips)], 1)

    def whole_pieces(buffer, half):
        return jnp.concatenate(
            [
                jnp.concatenate(
                    [buffer[half, across * row_tiles + down] for down in range(row_tiles)], 0
                )
                for across in range(chips // row_tiles)
            ],
            1,
        )

    def split_rows(source, high, low, span, column=0):
        step_rows = 2 * ROW_TILE
        half = high.shape[2]

        def one(step, carry):
            rows = pl.ds(pl.multiple_of(step * step_rows, step_rows), step_rows)
            for at in range(0, 2 * half, span):
                parity, place = (at // span) % 2, at // span // 2 * span
                upper, lower = split(source[rows, column + at : column + at + span])
                high[parity, rows, place : place + span] = upper
                low[parity, rows, place : place + span] = lower
            return carry

        lax.fori_loop(0, source.shape[0] // step_rows, one, 0)

    def fill_blocks(left, high, low):
        def fill(half, part):
            count, span = part.shape[0], part.shape[2]
            chunk = min(count * span, 512)
            for at in range(0, count * span, chunk):
                here = product(left, high[half, :, at : at + chunk], low[half, :, at : at + chunk])
                for block in range(chunk // span):
                    part[at // span + block] = here[:, block * span : (block + 1) * span]

        return fill

    def fill_pieces(left, high, low):
        def fill(half, part):
            here = product(left, high[half], low[half])
            for across in range(chips // row_tiles):
                for down in range(row_tiles):
                    part[across * row_tiles + down] = here[
                        down * ROW_TILE : (down + 1) * ROW_TILE,
                        across * piece : (across + 1) * piece,
                    ]

        return fill

    def gathered_product(phase, buffer, assemble, high, low):
        share_pair(phase, buffer)
        result = product(assemble(buffer, core), high[core], low[core], True)
        pair_arrived(phase, buffer)
        return result + product(assemble(buffer, other), high[other], low[other], True)

    live = live_blocks[0]
    for place in range(4):
        loads[place].wait()
    updates = []
    contributions = []
    for k in range(blocks_here):
        residual = leaf_right[:, k * width : (k + 1) * width]
        for child in range(k):
            residual = residual - jnp.where(parents[child] == k, updates[child], 0.0)
        block = jnp.where(k < live, product(residual, *split(leaf_inverse[k])), 0.0)
        solved[k] = block
        if k < blocks_here - 1:
            updates.append(product(block, *split(leaf_link[k])))
        contributions.append(product(block, *split(leaf_front[k])))
    spans = width // front_part
    for block in range(blocks_front):
        placed = jnp.zeros((columns, width), F32)
        for k in range(blocks_here):
            placed = placed + jnp.where(targets[k] == block, contributions[k], 0.0)
        for within in range(spans):
            owner = block * spans + within
            front_sum_part[owner % 2, owner // 2] = placed[
                :, within * front_part : (within + 1) * front_part
            ]

    pl.semaphore_wait(barrier, chips + groups - 1)
    send_pair(front_sum_part.at[other], front_sum_pair, FRONT_SUM)
    loads[4].wait()
    loads[5].wait()
    pair_done(FRONT_SUM, front_sum_part, front_sum_pair)
    chip_send(FRONT_SUM, front_sum_part, front_sum_got)

    split_rows(front_inverse, fi_high, fi_low, front_part)
    residual = front_right[...] - total(FRONT_SUM, front_sum_part, front_sum_got)
    pair_sum(FRONT_SOLVE, front_solve_part, front_solve_pair, fill_blocks(residual, fi_high, fi_low))
    pair_done(FRONT_SOLVE, front_solve_part, front_solve_pair)
    chip_send(FRONT_SOLVE, front_solve_part, front_solve_got)
    loads[6].wait()
    level_part = level_rows // devs
    for level in range(2):
        split_rows(
            front_couple, fc_high.at[level], fc_low.at[level], level_part, level * level_rows
        )
    front_forward = total(FRONT_SOLVE, front_solve_part, front_solve_got)

    pair_sum(
        RAISE_TOP,
        raise_top_part,
        raise_top_pair,
        fill_blocks(front_forward, fc_high.at[1], fc_low.at[1]),
    )
    pair_done(RAISE_TOP, raise_top_part, raise_top_pair)
    chip_send(RAISE_TOP, raise_top_part, raise_top_got)
    pair_sum(
        RAISE_LOW,
        raise_low_part,
        raise_low_pair,
        fill_blocks(front_forward, fc_high.at[0], fc_low.at[0]),
    )
    loads[7].wait()
    loads[8].wait()
    half = root_inverse.shape[2] // 2
    for level in (1, 0):
        split_rows(root_inverse.at[level], ri_high.at[level], ri_low.at[level], half)
    split_rows(root_couple.at[0], rc_high, rc_low, half)
    pair_done(RAISE_LOW, raise_low_part, raise_low_pair)
    raised_top = total(RAISE_TOP, raise_top_part, raise_top_got)
    share_grp(RAISE_TOP_GRP, raised_top, raise_top_grp)
    chip_send(RAISE_LOW, raise_low_part, raise_low_got)

    residual = root_right[:, 1, :] - total_grp(RAISE_TOP_GRP, raise_top_grp)
    pair_sum(TOP_SUM, top_part, top_pair, fill_pieces(residual, ri_high.at[1], ri_low.at[1]))
    pair_done(TOP_SUM, top_part, top_pair)
    chip_send(TOP_SUM, top_part, top_got)
    share_grp(RAISE_LOW_GRP, total(RAISE_LOW, raise_low_part, raise_low_got), raise_low_grp)
    share(TOP_SHARE, total(TOP_SUM, top_part, top_got), top_share)
    low_right = root_right[:, 0, :] - total_grp(RAISE_LOW_GRP, raise_low_grp)

    pushed = gathered_product(TOP_SHARE, top_share, whole_pieces, rc_high, rc_low)
    share_grp(PUSH_GRP, pushed, push_grp)
    residual = low_right - total_grp(PUSH_GRP, push_grp)
    pair_sum(LOW_SUM, low_part, low_pair, fill_pieces(residual, ri_high.at[0], ri_low.at[0]))
    pair_done(LOW_SUM, low_part, low_pair)
    chip_send(LOW_SUM, low_part, low_got)
    share(LOW_SHARE, total(LOW_SUM, low_part, low_got), low_share)

    back = gathered_product(LOW_SHARE, low_share, whole_pieces, ri_high.at[0], ri_low.at[0])
    share_grp(LOW_BACK_GRP, back, low_back_grp)
    low_solution = total_grp(LOW_BACK_GRP, low_back_grp)
    pair_sum(CORRECT_SUM, correct_part, correct_pair, fill_pieces(low_solution, rc_high, rc_low))
    pair_done(CORRECT_SUM, correct_part, correct_pair)
    chip_send(CORRECT_SUM, correct_part, correct_got)
    share(LOW_ALL, low_solution, low_all)
    root_out[:, 0, :] = low_solution
    share(CORRECT_SHARE, total(CORRECT_SUM, correct_part, correct_got), correct_share)
    lifted = gathered_product(LOW_ALL, low_all, whole, fc_high.at[0], fc_low.at[0])

    def corrected(buffer, side):
        return whole_pieces(top_share, side) - whole_pieces(buffer, side)

    back = gathered_product(CORRECT_SHARE, correct_share, corrected, ri_high.at[1], ri_low.at[1])
    share_grp(TOP_BACK_GRP, back, top_back_grp)
    top_solution = total_grp(TOP_BACK_GRP, top_back_grp)
    share(TOP_ALL, top_solution, top_all)
    root_out[:, 1, :] = top_solution

    lifted = lifted + gathered_product(TOP_ALL, top_all, whole, fc_high.at[1], fc_low.at[1])
    share(REMAINDER_ALL, front_forward - lifted, remainder_all)
    share(
        FRONT_ALL, gathered_product(REMAINDER_ALL, remainder_all, whole, fi_high, fi_low), front_all
    )
    share_pair(FRONT_ALL, front_all)
    pair_arrived(FRONT_ALL, front_all)
    for owner in range(devs):
        front_out[:, owner * front_part : (owner + 1) * front_part] = front_all[
            owner % 2, owner // 2
        ]

    solutions = [None] * blocks_here
    for k in reversed(range(blocks_here)):
        picked = jnp.zeros((columns, width), F32)
        for block in range(blocks_front):
            picked = picked + jnp.where(
                targets[k] == block, front_out[:, block * width : (block + 1) * width], 0.0
            )
        residual = solved[k] - product(picked, *split(leaf_front[k]), True)
        if k < blocks_here - 1:
            above = jnp.zeros((columns, width), F32)
            for upper in range(k + 1, blocks_here):
                above = above + jnp.where(parents[k] == upper, solutions[upper], 0.0)
            residual = residual - product(above, *split(leaf_link[k]), True)
        solutions[k] = jnp.where(k < live, product(residual, *split(leaf_inverse[k]), True), 0.0)
        leaf_out[:, k * width : (k + 1) * width] = solutions[k]

    for phase, buffer in (
        (FRONT_SUM, front_sum_part),
        (FRONT_SOLVE, front_solve_part),
        (RAISE_TOP, raise_top_part),
        (RAISE_LOW, raise_low_part),
        (TOP_SUM, top_part),
        (TOP_SHARE, top_share),
        (LOW_SUM, low_part),
        (LOW_SHARE, low_share),
        (CORRECT_SUM, correct_part),
        (CORRECT_SHARE, correct_share),
        (LOW_ALL, low_all),
        (TOP_ALL, top_all),
        (REMAINDER_ALL, remainder_all),
        (FRONT_ALL, front_all),
    ):
        settle(send_sem.at[phase], buffer.at[0, pl.ds(1, chips - 1)])
        settle(pair_send_sem.at[phase], buffer.at[0])
    for phase, buffer in (
        (RAISE_TOP_GRP, raise_top_grp),
        (RAISE_LOW_GRP, raise_low_grp),
        (PUSH_GRP, push_grp),
        (LOW_BACK_GRP, low_back_grp),
        (TOP_BACK_GRP, top_back_grp),
    ):
        settle(send_sem.at[phase], buffer.at[pl.ds(1, groups - 1)])


def body(
    groups,
    devs,
    leaf_right,
    leaf_inverse,
    leaf_link,
    leaf_front,
    parents,
    front_rows,
    live_blocks,
    front_right,
    front_inverse,
    front_couple,
    root_right,
    root_inverse,
    root_couple,
):
    columns = leaf_right.shape[0]
    front_part = front_right.shape[1]
    level_part = root_right.shape[2]
    level_columns = root_inverse.shape[2]
    row_tiles = columns // ROW_TILE
    piece = level_columns // 2 * row_tiles // (devs // 2)
    loaded = (
        leaf_right,
        leaf_inverse,
        leaf_link,
        leaf_front,
        front_right,
        front_inverse,
        front_couple,
        root_inverse,
        root_couple,
    )
    rows, half = front_inverse.shape[0], front_inverse.shape[1] // 2
    level_half = front_couple.shape[1] // 4
    root_rows, root_half = root_inverse.shape[1], level_columns // 2
    halves = (
        (2, rows, half),
        (2, 2, rows, level_half),
        (2, 2, root_rows, root_half),
        (2, root_rows, root_half),
    )
    chips = devs // 2
    front_full = pltpu.VMEM((2, chips, columns, front_part), F32)
    front_half = pltpu.VMEM((chips, columns, front_part), F32)
    level_full = pltpu.VMEM((2, chips, columns, level_part), F32)
    level_half_blocks = pltpu.VMEM((chips, columns, level_part), F32)
    pieces_full = pltpu.VMEM((2, chips, ROW_TILE, piece), F32)
    pieces_half = pltpu.VMEM((chips, ROW_TILE, piece), F32)
    grp_blocks = pltpu.VMEM((groups, columns, level_part), F32)
    vmem = pl.BlockSpec(memory_space=pltpu.VMEM)
    smem = pl.BlockSpec(memory_space=pltpu.SMEM)
    anywhere = pl.BlockSpec(memory_space=pl.ANY)
    return pl.pallas_call(
        functools.partial(kernel, groups, devs),
        out_shape=(
            jax.ShapeDtypeStruct(leaf_right.shape, F32),
            jax.ShapeDtypeStruct((columns, front_part * devs), F32),
            jax.ShapeDtypeStruct(root_right.shape, F32),
        ),
        in_specs=[smem] * 3 + [vmem] + [anywhere] * len(loaded),
        out_specs=(vmem, vmem, vmem),
        scratch_shapes=[pltpu.VMEM(array.shape, F32) for array in loaded]
        + [pltpu.VMEM(shape, BF16) for shape in halves for _ in range(2)]
        + [pltpu.VMEM((leaf_inverse.shape[0], columns, leaf_inverse.shape[1]), F32)]
        + [front_full] * 2
        + [front_half] * 4
        + [level_full] * 2
        + [level_half_blocks] * 4
        + [pieces_full] * 6
        + [pieces_half] * 6
        + [grp_blocks] * 5
        + [level_full] * 2
        + [front_full] * 2
        + [
            pltpu.SemaphoreType.DMA((len(loaded),)),
        ]
        + [pltpu.SemaphoreType.DMA((PHASES,))] * 4,
        compiler_params=pltpu.CompilerParams(
            collective_id=0, has_side_effects=True, vmem_limit_bytes=62 * 1024 * 1024
        ),
        name="block_solves",
    )(parents, front_rows, live_blocks, root_right, *loaded)


def solution(mesh):
    in_specs = (
        P(None, ("grp", "dev")),
        P(("grp", "dev"), None, None),
        P(("grp", "dev"), None, None),
        P(("grp", "dev"), None, None),
        P(("grp", "dev")),
        P(("grp", "dev")),
        P(("grp", "dev")),
        P(None, ("grp", "dev")),
        P(("grp", "dev"), None),
        P(("grp", "dev"), None),
        P(None, None, "dev"),
        P(None, "dev", "grp"),
        P(None, "dev", "grp"),
    )
    out_specs = (P(None, ("grp", "dev")), P(None, "grp"), P(None, None, "dev"))
    return jax.shard_map(
        functools.partial(body, mesh.shape["grp"], mesh.shape["dev"]),
        mesh=mesh,
        in_specs=in_specs,
        out_specs=out_specs,
        check_vma=False,
    )
```

time: 115 us -> 91.8 us (0.80)
  Pallas kernels: 99.3 us -> 85.8 us
  local copies, waits for them, and re-layouts: 13.3 us -> 4.42 us
    pallas_call x1, Pallas kernels: 99.3 us -> 85.8 us  [body(): pl.pallas_call(functools.partial(kernel, groups, devs), out_shape=(jax.Sh...]
    unnamed x27 -> x3, local copies, waits for them, and re-layouts: 13.3 us -> 4.42 us
where the time goes in v2:
time: 91.8 us; the launch traced here: 91.5 us
  Pallas kernels  85.8 us (93%)
  local copies, waits for them, and re-layouts  4.42 us (5%)
  between operations  1.29 us (1%)
    pallas_call x1, Pallas kernels, body(): pl.pallas_call(functools.partial(kernel, groups, devs), out_shape=(jax.Sh...  85.8 us
    unnamed x3, local copies, waits for them, and re-layouts  4.42 us

profile of v2, /device:TPU:1, one launch (start us, length us, event | category | flops | bytes accessed | tf_op | source)
XLA Modules:
  0.0 91.5 jit_solution(10286887858131126334)
XLA Ops:
  1.3 85.8 %block_solves.1 = (f32[32,256]{1,0:T(8,128)}, f32[32,2048]{1,0:T(8,128)}, f32[32,2,128]{2,1,0:T(2,128)}) custom-call(s32[2]{0:T(128)} %parents.1, s32[2]{0:T(128)} %targets.1, s32[1]{0:T(128)S(6)} %copy.19.live_blocks, f32[32,2,128]{2,1,0:T(2,128)} %root_right.1, f32[32,256]{1,0:T(8,128)} %leaf_right_hbm.1, f32[2,128,128]{2,1,0:T(8,128)} %leaf_inverse_hbm.1, ...), custom_call_target="tpu_custom_call" | custom-call | tf_op jit(solution)/shard_map/block_solves/pallas_call | solution.py:525
  87.0 1.4 %copy.20 = f32[32,256]{1,0:T(8,128)} copy(f32[32,256]{1,0:T(8,128)} %get-tuple-element.6) | data formatting | bytes 65536
  88.4 1.7 %copy.21 = f32[32,2048]{1,0:T(8,128)} copy(f32[32,2048]{1,0:T(8,128)} %get-tuple-element.7) | data formatting | bytes 524288
  90.1 1.4 %copy.22 = f32[32,2,128]{2,1,0:T(2,128)} copy(f32[32,2,128]{2,1,0:T(2,128)} %get-tuple-element.8) | data formatting | bytes 65536

commit v3 on v2

v3 whole, which is shorter than its diff:
```python
import functools

import jax
import jax.numpy as jnp
from jax import lax
from jax.experimental import pallas as pl
from jax.experimental.pallas import tpu as pltpu
from jax.sharding import PartitionSpec as P

MESH = pl.DeviceIdType.MESH
ROW_TILE = 8
F32 = jnp.float32
BF16 = jnp.bfloat16

(
    FRONT_SUM,
    FRONT_SOLVE,
    RAISE_TOP,
    RAISE_LOW,
    RAISE_TOP_QUAD,
    RAISE_LOW_QUAD,
    TOP_SUM,
    TOP_SHARE,
    PUSH_QUAD,
    LOW_SUM,
    LOW_SHARE,
    LOW_BACK_QUAD,
    CORRECT_SUM,
    CORRECT_SHARE,
    LOW_ALL,
    TOP_BACK_QUAD,
    TOP_ALL,
    REMAINDER_ALL,
    FRONT_ALL,
    ROOT_SWAP,
    PHASES,
) = range(21)


def split(values):
    high = values.astype(BF16)
    return high, (values - high.astype(F32)).astype(BF16)


def product(left, stacked):
    rows = left.shape[0]
    high, low = split(left)
    both = jnp.concatenate(
        [jnp.concatenate([high, high], 1), jnp.concatenate([low, low], 1)], 0
    )
    result = jnp.dot(both, stacked, preferred_element_type=F32)
    return result[:rows] + result[rows:]


def product_transposed(left, stacked):
    rows, depth = left.shape[0], stacked.shape[0] // 2
    result = lax.dot_general(
        jnp.concatenate(split(left), 0),
        stacked,
        (((1,), (1,)), ((), ())),
        preferred_element_type=F32,
    )
    result = result[:rows] + result[rows:]
    return result[:, :depth] + result[:, depth:]


def stack(values):
    return jnp.concatenate(split(values), 0)


def kernel(
    groups,
    devs,
    parents,
    targets,
    live_blocks,
    root_right,
    leaf_right_hbm,
    leaf_inverse_hbm,
    leaf_link_hbm,
    leaf_front_hbm,
    front_right_hbm,
    front_inverse_hbm,
    front_couple_hbm,
    root_inverse_hbm,
    root_couple_hbm,
    leaf_out,
    front_out,
    root_out,
    leaf_right,
    leaf_inverse,
    leaf_link,
    leaf_front,
    front_right,
    front_inverse,
    front_couple,
    root_halves,
    fi_stacked,
    fc_stacked,
    root_stacked,
    solved,
    front_sum_part,
    front_solve_part,
    front_sum_pair,
    front_sum_got,
    front_solve_pair,
    front_solve_got,
    raise_top_part,
    raise_low_part,
    raise_top_pair,
    raise_top_got,
    raise_low_pair,
    raise_low_got,
    top_part,
    low_part,
    correct_part,
    top_got,
    low_got,
    correct_got,
    top_share,
    low_share,
    correct_share,
    raise_top_quad,
    raise_low_quad,
    push_quad,
    low_back_quad,
    top_back_quad,
    low_all,
    top_all,
    remainder_all,
    front_all,
    load_sem,
    send_sem,
    recv_sem,
    pair_send_sem,
    pair_recv_sem,
):
    group = lax.axis_index("grp")
    me = lax.axis_index("dev")
    chips = devs // 2
    chip = me // 2
    core = lax.rem(me, 2)
    other = 1 - core
    sibling = (group, chip * 2 + other)
    quad = group * 2 + core
    columns = leaf_right.shape[0]
    blocks_here, width = leaf_inverse.shape[0], leaf_inverse.shape[1]
    blocks_front = front_inverse.shape[1] // width
    front_part = front_right.shape[1]
    level_rows = front_couple.shape[1] // 2
    row_tiles = columns // ROW_TILE
    piece = top_part.shape[2]
    half = root_halves.shape[3]
    quads = 2 * groups
    low_inverse, top_inverse, couple = range(3)

    def chip_peer(step):
        return (group, lax.rem(chip + step, chips) * 2 + core)

    def quad_peer(step):
        peer = lax.rem(quad + step, quads)
        return (peer // 2, chip * 2 + lax.rem(peer, 2))

    def half_of(matrix, side):
        columns_of = pl.ds(pl.multiple_of(side * half, half), half)
        if matrix == couple:
            return root_couple_hbm.at[0, :, columns_of]
        return root_inverse_hbm.at[matrix, :, columns_of]

    loads = [
        pltpu.make_async_copy(source, target, load_sem.at[place])
        for place, (source, target) in enumerate(
            (
                (leaf_right_hbm, leaf_right),
                (leaf_inverse_hbm, leaf_inverse),
                (leaf_link_hbm, leaf_link),
                (leaf_front_hbm, leaf_front),
                (front_right_hbm, front_right),
                (front_inverse_hbm, front_inverse),
                (front_couple_hbm, front_couple),
                (half_of(low_inverse, core), root_halves.at[low_inverse, core]),
                (half_of(top_inverse, core), root_halves.at[top_inverse, core]),
                (half_of(couple, core), root_halves.at[couple, core]),
            )
        )
    ]
    for load in loads:
        load.start()

    barrier = pltpu.get_barrier_semaphore()

    def greet(device):
        pl.semaphore_signal(barrier, inc=1, device_id=device, device_id_type=MESH)

    for step in range(1, chips):
        greet(chip_peer(step))
    for step in range(1, quads):
        greet(quad_peer(step))

    def send(source, target, device, phase):
        pltpu.make_async_remote_copy(
            src_ref=source,
            dst_ref=target,
            send_sem=send_sem.at[phase],
            recv_sem=recv_sem.at[phase],
            device_id=device,
            device_id_type=MESH,
        ).start()

    def send_pair(source, target, phase):
        pltpu.make_async_remote_copy(
            src_ref=source,
            dst_ref=target,
            send_sem=pair_send_sem.at[phase],
            recv_sem=pair_recv_sem.at[phase],
            device_id=sibling,
            device_id_type=MESH,
        ).start()

    def settle(semaphore, some):
        pltpu.make_async_copy(some, some, semaphore).wait()

    def pair_sum(phase, part, pair, fill):
        fill(other, part.at[other])
        send_pair(part.at[other], pair, phase)
        fill(core, part.at[core])

    def chip_send(phase, part, got):
        for step in range(1, chips):
            peer = lax.rem(chip + step, chips)
            send(part.at[core, peer], got.at[step], chip_peer(step), phase)

    def pair_done(phase, part, pair):
        settle(pair_recv_sem.at[phase], pair)
        for place in range(chips):
            part[core, place] = part[core, place] + pair[place]

    def total(phase, part, got):
        result = part[core, chip]
        settle(recv_sem.at[phase], got.at[pl.ds(1, chips - 1)])
        for place in range(1, chips):
            result = result + got[place]
        return result

    def share(phase, values, buffer):
        buffer[core, chip] = values
        for step in range(1, chips):
            send(buffer.at[core, chip], buffer.at[core, chip], chip_peer(step), phase)

    def share_pair(phase, buffer):
        settle(recv_sem.at[phase], buffer.at[0, pl.ds(1, chips - 1)])
        send_pair(buffer.at[core], buffer.at[core], phase)

    def pair_arrived(phase, buffer):
        settle(pair_recv_sem.at[phase], buffer.at[0])

    def share_quad(phase, values, buffer):
        buffer[quad] = values
        for step in range(1, quads):
            send(buffer.at[quad], buffer.at[quad], quad_peer(step), phase)

    def quad_wait(phase, buffer):
        settle(recv_sem.at[phase], buffer.at[pl.ds(1, quads - 1)])

    def total_quad(phase, buffer):
        quad_wait(phase, buffer)
        result = buffer[0]
        for place in range(1, quads):
            result = result + buffer[place]
        return result

    def pair_quad(phase, buffer):
        quad_wait(phase, buffer)
        sides = []
        for side in range(2):
            result = buffer[side]
            for place in range(1, groups):
                result = result + buffer[2 * place + side]
            sides.append(result)
        return jnp.concatenate(sides, 1)

    def own_side(values):
        part = values.shape[1] // 2
        return jnp.where(core == 0, values[:, :part], values[:, part:])

    def whole(buffer, side):
        return jnp.concatenate([buffer[side, place] for place in range(chips)], 1)

    def split_rows(source, stacked, span, column=0):
        step_rows = 2 * ROW_TILE
        count = source.shape[0]

        def one(step, carry):
            at_rows = pl.multiple_of(step * step_rows, step_rows)
            rows = pl.ds(at_rows, step_rows)
            rows_low = pl.ds(pl.multiple_of(at_rows + count, step_rows), step_rows)
            for at in range(0, 2 * stacked.shape[2], span):
                parity, place = (at // span) % 2, at // span // 2 * span
                upper, lower = split(source[rows, column + at : column + at + span])
                stacked[parity, rows, place : place + span] = upper
                stacked[parity, rows_low, place : place + span] = lower
            return carry

        lax.fori_loop(0, count // step_rows, one, 0)

    def split_root(matrix):
        step_rows = 2 * ROW_TILE
        count = root_halves.shape[2]

        def one(step, carry):
            at_rows = pl.multiple_of(step * step_rows, step_rows)
            for side in range(2):
                upper, lower = split(root_halves[matrix, side, pl.ds(at_rows, step_rows), :])
                for start, values in ((side, upper), (side + 2, lower)):
                    rows = pl.multiple_of(at_rows + start * count, step_rows)
                    root_stacked[matrix, pl.ds(rows, step_rows), :] = values
            return carry

        lax.fori_loop(0, count // step_rows, one, 0)

    def fill_blocks(left, stacked):
        def fill(side, part):
            count, span = part.shape[0], part.shape[2]
            chunk = min(count * span, 512)
            for at in range(0, count * span, chunk):
                here = product(left, stacked[side, :, at : at + chunk])
                for block in range(chunk // span):
                    part[at // span + block] = here[:, block * span : (block + 1) * span]

        return fill

    def send_pieces(phase, values, part, got):
        for across in range(chips // row_tiles):
            for down in range(row_tiles):
                part[across * row_tiles + down] = values[
                    down * ROW_TILE : (down + 1) * ROW_TILE,
                    across * piece : (across + 1) * piece,
                ]
        for step in range(1, chips):
            send(part.at[lax.rem(chip + step, chips)], got.at[step], chip_peer(step), phase)

    def share_pieces(phase, share_phase, part, got, buffer):
        settle(recv_sem.at[phase], got.at[pl.ds(1, chips - 1)])
        result = part[chip]
        for place in range(1, chips):
            result = result + got[place]
        buffer[chip] = result
        for step in range(1, chips):
            send(buffer.at[chip], buffer.at[chip], chip_peer(step), share_phase)

    def whole_pieces(buffer):
        return jnp.concatenate(
            [
                jnp.concatenate([buffer[across * row_tiles + down] for down in range(row_tiles)], 0)
                for across in range(chips // row_tiles)
            ],
            1,
        )

    def shared_pieces(phase, buffer):
        settle(recv_sem.at[phase], buffer.at[pl.ds(1, chips - 1)])
        return whole_pieces(buffer)

    def half_product(buffer, stacked, side):
        return product_transposed(whole(buffer, side), stacked[side])

    def gathered_product(phase, buffer, stacked):
        share_pair(phase, buffer)
        result = half_product(buffer, stacked, core)
        pair_arrived(phase, buffer)
        return result + half_product(buffer, stacked, other)

    live = live_blocks[0]
    for place in range(4):
        loads[place].wait()
    updates = []
    contributions = []
    for k in range(blocks_here):
        residual = leaf_right[:, k * width : (k + 1) * width]
        for child in range(k):
            residual = residual - jnp.where(parents[child] == k, updates[child], 0.0)
        block = jnp.where(k < live, product(residual, stack(leaf_inverse[k])), 0.0)
        solved[k] = block
        if k < blocks_here - 1:
            updates.append(product(block, stack(leaf_link[k])))
        contributions.append(product(block, stack(leaf_front[k])))
    spans = width // front_part
    for block in range(blocks_front):
        placed = jnp.zeros((columns, width), F32)
        for k in range(blocks_here):
            placed = placed + jnp.where(targets[k] == block, contributions[k], 0.0)
        for within in range(spans):
            owner = block * spans + within
            front_sum_part[owner % 2, owner // 2] = placed[
                :, within * front_part : (within + 1) * front_part
            ]

    pl.semaphore_wait(barrier, chips - 1 + quads - 1)
    send_pair(front_sum_part.at[other], front_sum_pair, FRONT_SUM)
    for matrix in range(3):
        send_pair(half_of(matrix, other), root_halves.at[matrix, core], ROOT_SWAP)
    loads[4].wait()
    loads[5].wait()
    pair_done(FRONT_SUM, front_sum_part, front_sum_pair)
    chip_send(FRONT_SUM, front_sum_part, front_sum_got)

    split_rows(front_inverse, fi_stacked, front_part)
    residual = front_right[...] - total(FRONT_SUM, front_sum_part, front_sum_got)
    pair_sum(FRONT_SOLVE, front_solve_part, front_solve_pair, fill_blocks(residual, fi_stacked))
    pair_done(FRONT_SOLVE, front_solve_part, front_solve_pair)
    chip_send(FRONT_SOLVE, front_solve_part, front_solve_got)
    loads[6].wait()
    level_part = level_rows // devs
    for level in range(2):
        split_rows(front_couple, fc_stacked.at[level], level_part, level * level_rows)
    front_forward = total(FRONT_SOLVE, front_solve_part, front_solve_got)

    pair_sum(
        RAISE_TOP, raise_top_part, raise_top_pair, fill_blocks(front_forward, fc_stacked.at[1])
    )
    pair_done(RAISE_TOP, raise_top_part, raise_top_pair)
    chip_send(RAISE_TOP, raise_top_part, raise_top_got)
    pair_sum(
        RAISE_LOW, raise_low_part, raise_low_pair, fill_blocks(front_forward, fc_stacked.at[0])
    )
    for place in (7, 8, 9):
        loads[place].wait()
    settle(pair_recv_sem.at[ROOT_SWAP], root_halves.at[:, 0])
    for matrix in range(3):
        split_root(matrix)
    pair_done(RAISE_LOW, raise_low_part, raise_low_pair)

    def less_right(level, values):
        return values - jnp.where(group == 0, root_right[:, level, :], 0.0)

    raised_top = total(RAISE_TOP, raise_top_part, raise_top_got)
    share_quad(RAISE_TOP_QUAD, less_right(1, raised_top), raise_top_quad)
    chip_send(RAISE_LOW, raise_low_part, raise_low_got)

    residual = -pair_quad(RAISE_TOP_QUAD, raise_top_quad)
    send_pieces(TOP_SUM, product(residual, root_stacked[top_inverse]), top_part, top_got)
    raised_low = total(RAISE_LOW, raise_low_part, raise_low_got)
    share_quad(RAISE_LOW_QUAD, less_right(0, raised_low), raise_low_quad)
    share_pieces(TOP_SUM, TOP_SHARE, top_part, top_got, top_share)
    low_right = -pair_quad(RAISE_LOW_QUAD, raise_low_quad)

    top_forward = shared_pieces(TOP_SHARE, top_share)
    share_quad(PUSH_QUAD, product_transposed(top_forward, root_stacked[couple]), push_quad)
    residual = low_right - total_quad(PUSH_QUAD, push_quad)
    send_pieces(LOW_SUM, product(residual, root_stacked[low_inverse]), low_part, low_got)
    share_pieces(LOW_SUM, LOW_SHARE, low_part, low_got, low_share)

    low_forward = shared_pieces(LOW_SHARE, low_share)
    back = product_transposed(low_forward, root_stacked[low_inverse])
    share_quad(LOW_BACK_QUAD, back, low_back_quad)
    low_pair = total_quad(LOW_BACK_QUAD, low_back_quad)
    send_pieces(CORRECT_SUM, product(low_pair, root_stacked[couple]), correct_part, correct_got)
    low_solution = own_side(low_pair)
    root_out[:, 0, :] = low_solution
    share_pieces(CORRECT_SUM, CORRECT_SHARE, correct_part, correct_got, correct_share)
    share(LOW_ALL, low_solution, low_all)
    residual = whole_pieces(top_share) - shared_pieces(CORRECT_SHARE, correct_share)
    back = product_transposed(residual, root_stacked[top_inverse])
    share_quad(TOP_BACK_QUAD, back, top_back_quad)
    share_pair(LOW_ALL, low_all)
    top_solution = own_side(total_quad(TOP_BACK_QUAD, top_back_quad))
    share(TOP_ALL, top_solution, top_all)
    root_out[:, 1, :] = top_solution
    lifted = half_product(low_all, fc_stacked.at[0], core)
    pair_arrived(LOW_ALL, low_all)
    lifted = lifted + half_product(low_all, fc_stacked.at[0], other)

    lifted = lifted + gathered_product(TOP_ALL, top_all, fc_stacked.at[1])
    share(REMAINDER_ALL, front_forward - lifted, remainder_all)
    share(FRONT_ALL, gathered_product(REMAINDER_ALL, remainder_all, fi_stacked), front_all)
    share_pair(FRONT_ALL, front_all)
    pair_arrived(FRONT_ALL, front_all)
    for owner in range(devs):
        front_out[:, owner * front_part : (owner + 1) * front_part] = front_all[
            owner % 2, owner // 2
        ]

    solutions = [None] * blocks_here
    for k in reversed(range(blocks_here)):
        picked = jnp.zeros((columns, width), F32)
        for block in range(blocks_front):
            picked = picked + jnp.where(
                targets[k] == block, front_out[:, block * width : (block + 1) * width], 0.0
            )
        residual = solved[k] - product_transposed(picked, stack(leaf_front[k]))
        if k < blocks_here - 1:
            above = jnp.zeros((columns, width), F32)
            for upper in range(k + 1, blocks_here):
                above = above + jnp.where(parents[k] == upper, solutions[upper], 0.0)
            residual = residual - product_transposed(above, stack(leaf_link[k]))
        solutions[k] = jnp.where(k < live, product_transposed(residual, stack(leaf_inverse[k])), 0.0)
        leaf_out[:, k * width : (k + 1) * width] = solutions[k]

    for phase, buffer in (
        (FRONT_SUM, front_sum_part),
        (FRONT_SOLVE, front_solve_part),
        (RAISE_TOP, raise_top_part),
        (RAISE_LOW, raise_low_part),
        (LOW_ALL, low_all),
        (TOP_ALL, top_all),
        (REMAINDER_ALL, remainder_all),
        (FRONT_ALL, front_all),
    ):
        settle(send_sem.at[phase], buffer.at[0, pl.ds(1, chips - 1)])
        settle(pair_send_sem.at[phase], buffer.at[0])
    for phase, buffer in (
        (TOP_SUM, top_part),
        (TOP_SHARE, top_share),
        (LOW_SUM, low_part),
        (LOW_SHARE, low_share),
        (CORRECT_SUM, correct_part),
        (CORRECT_SHARE, correct_share),
    ):
        settle(send_sem.at[phase], buffer.at[pl.ds(1, chips - 1)])
    for phase, buffer in (
        (RAISE_TOP_QUAD, raise_top_quad),
        (RAISE_LOW_QUAD, raise_low_quad),
        (PUSH_QUAD, push_quad),
        (LOW_BACK_QUAD, low_back_quad),
        (TOP_BACK_QUAD, top_back_quad),
    ):
        settle(send_sem.at[phase], buffer.at[pl.ds(1, quads - 1)])
    settle(pair_send_sem.at[ROOT_SWAP], root_halves.at[:, 0])


def hand_on(*refs):
    semaphores = refs[-1]
    count = (len(refs) - 1) // 2
    copies = [
        pltpu.make_async_copy(refs[place], refs[count + place], semaphores.at[place])
        for place in range(count)
    ]
    for copy in copies:
        copy.start()
    for copy in copies:
        copy.wait()


def body(
    groups,
    devs,
    leaf_right,
    leaf_inverse,
    leaf_link,
    leaf_front,
    parents,
    front_rows,
    live_blocks,
    front_right,
    front_inverse,
    front_couple,
    root_right,
    root_inverse,
    root_couple,
):
    columns = leaf_right.shape[0]
    front_part = front_right.shape[1]
    level_part = root_right.shape[2]
    level_columns = root_inverse.shape[2]
    row_tiles = columns // ROW_TILE
    piece = level_columns // 2 * row_tiles // (devs // 2)
    loaded = (
        leaf_right,
        leaf_inverse,
        leaf_link,
        leaf_front,
        front_right,
        front_inverse,
        front_couple,
        root_inverse,
        root_couple,
    )
    rows, half = front_inverse.shape[0], front_inverse.shape[1] // 2
    level_half = front_couple.shape[1] // 4
    root_rows, root_half = root_inverse.shape[1], level_columns // 2
    halves = (
        (2, 2 * rows, half),
        (2, 2, 2 * rows, level_half),
        (3, 4 * root_rows, root_half),
    )
    chips = devs // 2
    front_full = pltpu.VMEM((2, chips, columns, front_part), F32)
    front_half = pltpu.VMEM((chips, columns, front_part), F32)
    level_full = pltpu.VMEM((2, chips, columns, level_part), F32)
    level_half_blocks = pltpu.VMEM((chips, columns, level_part), F32)
    pieces_half = pltpu.VMEM((chips, ROW_TILE, piece), F32)
    quad_blocks = pltpu.VMEM((2 * groups, columns, level_part), F32)
    quad_pairs = pltpu.VMEM((2 * groups, columns, 2 * level_part), F32)
    vmem = pl.BlockSpec(memory_space=pltpu.VMEM)
    smem = pl.BlockSpec(memory_space=pltpu.SMEM)
    anywhere = pl.BlockSpec(memory_space=pl.ANY)
    results = (
        jax.ShapeDtypeStruct(leaf_right.shape, F32),
        jax.ShapeDtypeStruct((columns, front_part * devs), F32),
        jax.ShapeDtypeStruct(root_right.shape, F32),
    )
    solutions = pl.pallas_call(
        functools.partial(kernel, groups, devs),
        out_shape=results,
        in_specs=[smem] * 3 + [vmem] + [anywhere] * len(loaded),
        out_specs=(vmem, vmem, vmem),
        scratch_shapes=[pltpu.VMEM(array.shape, F32) for array in loaded[:-2]]
        + [pltpu.VMEM((3, 2, root_rows, root_half), F32)]
        + [pltpu.VMEM(shape, BF16) for shape in halves]
        + [pltpu.VMEM((leaf_inverse.shape[0], columns, leaf_inverse.shape[1]), F32)]
        + [front_full] * 2
        + [front_half] * 4
        + [level_full] * 2
        + [level_half_blocks] * 4
        + [pieces_half] * 9
        + [quad_blocks] * 2
        + [quad_pairs] * 3
        + [level_full] * 2
        + [front_full] * 2
        + [
            pltpu.SemaphoreType.DMA((len(loaded) + 1,)),
        ]
        + [pltpu.SemaphoreType.DMA((PHASES,))] * 4,
        compiler_params=pltpu.CompilerParams(
            collective_id=0, has_side_effects=True, vmem_limit_bytes=62 * 1024 * 1024
        ),
        name="block_solves",
    )(parents, front_rows, live_blocks, root_right, *loaded)
    return pl.pallas_call(
        hand_on,
        out_shape=results,
        in_specs=[anywhere] * len(results),
        out_specs=(anywhere,) * len(results),
        scratch_shapes=[pltpu.SemaphoreType.DMA((len(results),))],
        compiler_params=pltpu.CompilerParams(vmem_limit_bytes=62 * 1024 * 1024),
        name="hand_on",
    )(*solutions)


def solution(mesh):
    in_specs = (
        P(None, ("grp", "dev")),
        P(("grp", "dev"), None, None),
        P(("grp", "dev"), None, None),
        P(("grp", "dev"), None, None),
        P(("grp", "dev")),
        P(("grp", "dev")),
        P(("grp", "dev")),
        P(None, ("grp", "dev")),
        P(("grp", "dev"), None),
        P(("grp", "dev"), None),
        P(None, None, "dev"),
        P(None, "dev", "grp"),
        P(None, "dev", "grp"),
    )
    out_specs = (P(None, ("grp", "dev")), P(None, "grp"), P(None, None, "dev"))
    return jax.shard_map(
        functools.partial(body, mesh.shape["grp"], mesh.shape["dev"]),
        mesh=mesh,
        in_specs=in_specs,
        out_specs=out_specs,
        check_vma=False,
    )
```

time: 91.8 us -> 97.7 us (1.064)
  Pallas kernels: 85.8 us -> 96.2 us
  local copies, waits for them, and re-layouts: 4.42 us -> 0 us
    pallas_call x1 -> x2, Pallas kernels: 85.8 us -> 96.2 us  [the longest x1 85.1 us: body(): pl.pallas_call(functools.partial(kernel, groups, devs), out_shape=results...]
    unnamed x3 -> x0, local copies, waits for them, and re-layouts: 4.42 us -> none
where the time goes in v3:
time: 97.7 us; the launch traced here: 97.5 us
  Pallas kernels  96.2 us (98%)
  between operations  1.29 us (1%)
    pallas_call x1, Pallas kernels, body(): pl.pallas_call(functools.partial(kernel, groups, devs), out_shape=results...  85.1 us
    pallas_call x1, Pallas kernels, body(): pl.pallas_call(hand_on, out_shape=results, in_specs=[anywhere] * len(resu...  11.1 us

profile of v3, /device:TPU:1, one launch (start us, length us, event | category | flops | bytes accessed | tf_op | source)
XLA Modules:
  0.0 97.5 jit_solution(9841244637236788461)
XLA Ops:
  1.3 85.1 %block_solves.1 = (f32[32,256]{1,0:T(8,128)}, f32[32,2048]{1,0:T(8,128)}, f32[32,2,128]{2,1,0:T(2,128)}) custom-call(s32[2]{0:T(128)} %parents.1, s32[2]{0:T(128)} %targets.1, s32[1]{0:T(128)S(6)} %copy.16.live_blocks, f32[32,2,128]{2,1,0:T(2,128)} %root_right.1, f32[32,256]{1,0:T(8,128)} %leaf_right_hbm.1, f32[2,128,128]{2,1,0:T(8,128)} %leaf_inverse_hbm.1, ...), custom_call_target="tpu_custom_call" | custom-call | tf_op jit(solution)/shard_map/block_solves/pallas_call | solution.py:602
  86.4 11.1 %hand_on.1 = (f32[32,256]{1,0:T(8,128)}, f32[32,2048]{1,0:T(8,128)}, f32[32,2,128]{2,1,0:T(2,128)}) custom-call(f32[32,256]{1,0:T(8,128)} %get-tuple-element.6.refs_0_, f32[32,2048]{1,0:T(8,128)} %get-tuple-element.7.refs_1_, f32[32,2,128]{2,1,0:T(2,128)} %get-tuple-element.8.refs_2_), custom_call_target="tpu_custom_call" | custom-call | tf_op jit(solution)/shard_map/hand_on/pallas_call | solution.py:629

commit v4 on v0

v4 whole, which is shorter than its diff:
```python
import functools

import jax
import jax.numpy as jnp
from jax import lax
from jax.experimental import pallas as pl
from jax.experimental.pallas import tpu as pltpu
from jax.sharding import PartitionSpec as P

MESH = pl.DeviceIdType.MESH
ROW_TILE = 8
STREAMS = 2
F32 = jnp.float32
BF16 = jnp.bfloat16

(
    FRONT_SUM,
    FRONT_SOLVE,
    RAISE_TOP,
    RAISE_LOW,
    RAISE_TOP_QUAD,
    RAISE_LOW_QUAD,
    TOP_SUM,
    TOP_SHARE,
    PUSH_QUAD,
    LOW_SUM,
    LOW_SHARE,
    LOW_BACK_QUAD,
    CORRECT_SUM,
    CORRECT_SHARE,
    LOW_ALL,
    TOP_BACK_QUAD,
    TOP_ALL,
    REMAINDER_ALL,
    FRONT_ALL,
    ROOT_SWAP,
    PHASES,
) = range(21)


def split(values):
    high = values.astype(BF16)
    return high, (values - high.astype(F32)).astype(BF16)


def product(left, stacked):
    rows = left.shape[0]
    high, low = split(left)
    both = jnp.concatenate(
        [jnp.concatenate([high, high], 1), jnp.concatenate([low, low], 1)], 0
    )
    result = jnp.dot(both, stacked, preferred_element_type=F32)
    return result[:rows] + result[rows:]


def product_transposed(left, stacked):
    rows, depth = left.shape[0], stacked.shape[0] // 2
    result = lax.dot_general(
        jnp.concatenate(split(left), 0),
        stacked,
        (((1,), (1,)), ((), ())),
        preferred_element_type=F32,
    )
    result = result[:rows] + result[rows:]
    return result[:, :depth] + result[:, depth:]


def stack(values):
    return jnp.concatenate(split(values), 0)


def kernel(
    groups,
    devs,
    parents,
    targets,
    live_blocks,
    root_right,
    leaf_right_hbm,
    leaf_inverse_hbm,
    leaf_link_hbm,
    leaf_front_hbm,
    front_right_hbm,
    front_inverse_hbm,
    front_couple_hbm,
    root_inverse_hbm,
    root_couple_hbm,
    leaf_out,
    front_out,
    root_out,
    leaf_right,
    leaf_inverse,
    leaf_link,
    leaf_front,
    front_right,
    front_inverse,
    front_couple,
    root_halves,
    fi_stacked,
    fc_stacked,
    root_stacked,
    *rest,
):
    *buffers, load_sem, send_sem, recv_sem, pair_send_sem, pair_recv_sem = rest
    group = lax.axis_index("grp")
    me = lax.axis_index("dev")
    chips = devs // 2
    chip = me // 2
    core = lax.rem(me, 2)
    other = 1 - core
    sibling = (group, chip * 2 + other)
    quad = group * 2 + core
    columns = leaf_right.shape[0] // STREAMS
    blocks_here, width = leaf_inverse.shape[0], leaf_inverse.shape[1]
    blocks_front = front_inverse.shape[1] // width
    front_part = front_right.shape[1]
    level_rows = front_couple.shape[1] // 2
    row_tiles = columns // ROW_TILE
    half = root_halves.shape[3]
    quads = 2 * groups
    piece = half * row_tiles // chips
    low_inverse, top_inverse, couple = range(3)

    def chip_peer(step):
        return (group, lax.rem(chip + step, chips) * 2 + core)

    def quad_peer(step):
        peer = lax.rem(quad + step, quads)
        return (peer // 2, chip * 2 + lax.rem(peer, 2))

    def half_of(matrix, side):
        columns_of = pl.ds(pl.multiple_of(side * half, half), half)
        if matrix == couple:
            return root_couple_hbm.at[0, :, columns_of]
        return root_inverse_hbm.at[matrix, :, columns_of]

    loads = [
        pltpu.make_async_copy(source, target, load_sem.at[place])
        for place, (source, target) in enumerate(
            (
                (leaf_right_hbm, leaf_right),
                (leaf_inverse_hbm, leaf_inverse),
                (leaf_link_hbm, leaf_link),
                (leaf_front_hbm, leaf_front),
                (front_right_hbm, front_right),
                (front_inverse_hbm, front_inverse),
                (front_couple_hbm, front_couple),
                (half_of(low_inverse, core), root_halves.at[low_inverse, core]),
                (half_of(top_inverse, core), root_halves.at[top_inverse, core]),
                (half_of(couple, core), root_halves.at[couple, core]),
            )
        )
    ]
    for load in loads:
        load.start()

    barrier = pltpu.get_barrier_semaphore()

    def greet(device):
        pl.semaphore_signal(barrier, inc=1, device_id=device, device_id_type=MESH)

    for step in range(1, chips):
        greet(chip_peer(step))
    for step in range(1, quads):
        greet(quad_peer(step))

    def solve(stream):
        own_rows = slice(stream * columns, (stream + 1) * columns)
        (
            solved,
            front_sum_part,
            front_solve_part,
            front_sum_pair,
            front_sum_got,
            front_solve_pair,
            front_solve_got,
            raise_top_part,
            raise_low_part,
            raise_top_pair,
            raise_top_got,
            raise_low_pair,
            raise_low_got,
            top_part,
            low_part,
            correct_part,
            top_got,
            low_got,
            correct_got,
            top_share,
            low_share,
            correct_share,
            raise_top_quad,
            raise_low_quad,
            push_quad,
            low_back_quad,
            top_back_quad,
            low_all,
            top_all,
            remainder_all,
            front_all,
        ) = [buffer.at[stream] for buffer in buffers]

        def send(source, target, device, phase):
            pltpu.make_async_remote_copy(
                src_ref=source,
                dst_ref=target,
                send_sem=send_sem.at[stream, phase],
                recv_sem=recv_sem.at[stream, phase],
                device_id=device,
                device_id_type=MESH,
            ).start()

        def send_pair(source, target, phase):
            pltpu.make_async_remote_copy(
                src_ref=source,
                dst_ref=target,
                send_sem=pair_send_sem.at[stream, phase],
                recv_sem=pair_recv_sem.at[stream, phase],
                device_id=sibling,
                device_id_type=MESH,
            ).start()

        def settle(semaphore, some):
            pltpu.make_async_copy(some, some, semaphore).wait()

        def pair_sum(phase, part, pair, fill):
            fill(other, part.at[other])
            send_pair(part.at[other], pair, phase)
            fill(core, part.at[core])

        def chip_send(phase, part, got):
            for step in range(1, chips):
                peer = lax.rem(chip + step, chips)
                send(part.at[core, peer], got.at[step], chip_peer(step), phase)

        def pair_done(phase, part, pair):
            settle(pair_recv_sem.at[stream, phase], pair)
            for place in range(chips):
                part[core, place] = part[core, place] + pair[place]

        def total(phase, part, got):
            result = part[core, chip]
            settle(recv_sem.at[stream, phase], got.at[pl.ds(1, chips - 1)])
            for place in range(1, chips):
                result = result + got[place]
            return result

        def share(phase, values, buffer):
            buffer[core, chip] = values
            for step in range(1, chips):
                send(buffer.at[core, chip], buffer.at[core, chip], chip_peer(step), phase)

        def share_pair(phase, buffer):
            settle(recv_sem.at[stream, phase], buffer.at[0, pl.ds(1, chips - 1)])
            send_pair(buffer.at[core], buffer.at[core], phase)

        def pair_arrived(phase, buffer):
            settle(pair_recv_sem.at[stream, phase], buffer.at[0])

        def share_quad(phase, values, buffer):
            buffer[quad] = values
            for step in range(1, quads):
                send(buffer.at[quad], buffer.at[quad], quad_peer(step), phase)

        def quad_wait(phase, buffer):
            settle(recv_sem.at[stream, phase], buffer.at[pl.ds(1, quads - 1)])

        def total_quad(phase, buffer):
            quad_wait(phase, buffer)
            result = buffer[0]
            for place in range(1, quads):
                result = result + buffer[place]
            return result

        def pair_quad(phase, buffer):
            quad_wait(phase, buffer)
            sides = []
            for side in range(2):
                result = buffer[side]
                for place in range(1, groups):
                    result = result + buffer[2 * place + side]
                sides.append(result)
            return jnp.concatenate(sides, 1)

        def own_side(values):
            part = values.shape[1] // 2
            return jnp.where(core == 0, values[:, :part], values[:, part:])

        def whole(buffer, side):
            return jnp.concatenate([buffer[side, place] for place in range(chips)], 1)

        def split_rows(source, stacked, span, column=0):
            step_rows = 2 * ROW_TILE
            count = source.shape[0]

            def one(step, carry):
                at_rows = pl.multiple_of(step * step_rows, step_rows)
                rows = pl.ds(at_rows, step_rows)
                rows_low = pl.ds(pl.multiple_of(at_rows + count, step_rows), step_rows)
                for at in range(0, 2 * stacked.shape[2], span):
                    parity, place = (at // span) % 2, at // span // 2 * span
                    upper, lower = split(source[rows, column + at : column + at + span])
                    stacked[parity, rows, place : place + span] = upper
                    stacked[parity, rows_low, place : place + span] = lower
                return carry

            lax.fori_loop(0, count // step_rows, one, 0)

        def split_root(matrix):
            step_rows = 2 * ROW_TILE
            count = root_halves.shape[2]

            def one(step, carry):
                at_rows = pl.multiple_of(step * step_rows, step_rows)
                for side in range(2):
                    upper, lower = split(root_halves[matrix, side, pl.ds(at_rows, step_rows), :])
                    for start, values in ((side, upper), (side + 2, lower)):
                        rows = pl.multiple_of(at_rows + start * count, step_rows)
                        root_stacked[matrix, pl.ds(rows, step_rows), :] = values
                return carry

            lax.fori_loop(0, count // step_rows, one, 0)

        def fill_blocks(left, stacked):
            def fill(side, part):
                count, span = part.shape[0], part.shape[2]
                chunk = min(count * span, 512)
                for at in range(0, count * span, chunk):
                    here = product(left, stacked[side, :, at : at + chunk])
                    for block in range(chunk // span):
                        part[at // span + block] = here[:, block * span : (block + 1) * span]

            return fill

        def send_pieces(phase, values, part, got):
            for across in range(chips // row_tiles):
                for down in range(row_tiles):
                    part[across * row_tiles + down] = values[
                        down * ROW_TILE : (down + 1) * ROW_TILE,
                        across * piece : (across + 1) * piece,
                    ]
            for step in range(1, chips):
                send(part.at[lax.rem(chip + step, chips)], got.at[step], chip_peer(step), phase)

        def share_pieces(phase, share_phase, part, got, buffer):
            settle(recv_sem.at[stream, phase], got.at[pl.ds(1, chips - 1)])
            result = part[chip]
            for place in range(1, chips):
                result = result + got[place]
            buffer[chip] = result
            for step in range(1, chips):
                send(buffer.at[chip], buffer.at[chip], chip_peer(step), share_phase)

        def whole_pieces(buffer):
            return jnp.concatenate(
                [
                    jnp.concatenate([buffer[across * row_tiles + down] for down in range(row_tiles)], 0)
                    for across in range(chips // row_tiles)
                ],
                1,
            )

        def shared_pieces(phase, buffer):
            settle(recv_sem.at[stream, phase], buffer.at[pl.ds(1, chips - 1)])
            return whole_pieces(buffer)

        def half_product(buffer, stacked, side):
            return product_transposed(whole(buffer, side), stacked[side])

        def gathered_product(phase, buffer, stacked):
            yield
            share_pair(phase, buffer)
            result = half_product(buffer, stacked, core)
            yield
            pair_arrived(phase, buffer)
            return result + half_product(buffer, stacked, other)

        live = live_blocks[0]
        if stream == 0:
            for place in range(4):
                loads[place].wait()
        updates = []
        contributions = []
        for k in range(blocks_here):
            residual = leaf_right[own_rows, k * width : (k + 1) * width]
            for child in range(k):
                residual = residual - jnp.where(parents[child] == k, updates[child], 0.0)
            block = jnp.where(k < live, product(residual, stack(leaf_inverse[k])), 0.0)
            solved[k] = block
            if k < blocks_here - 1:
                updates.append(product(block, stack(leaf_link[k])))
            contributions.append(product(block, stack(leaf_front[k])))
        spans = width // front_part
        for block in range(blocks_front):
            placed = jnp.zeros((columns, width), F32)
            for k in range(blocks_here):
                placed = placed + jnp.where(targets[k] == block, contributions[k], 0.0)
            for within in range(spans):
                owner = block * spans + within
                front_sum_part[owner % 2, owner // 2] = placed[
                    :, within * front_part : (within + 1) * front_part
                ]

        if stream == 0:
            pl.semaphore_wait(barrier, chips - 1 + quads - 1)
        send_pair(front_sum_part.at[other], front_sum_pair, FRONT_SUM)
        yield
        if stream == 0:
            loads[4].wait()
            loads[5].wait()
        pair_done(FRONT_SUM, front_sum_part, front_sum_pair)
        chip_send(FRONT_SUM, front_sum_part, front_sum_got)

        if stream == 0:
            split_rows(front_inverse, fi_stacked, front_part)
            for matrix in range(3):
                send_pair(half_of(matrix, other), root_halves.at[matrix, core], ROOT_SWAP)
        yield
        residual = front_right[own_rows, :] - total(FRONT_SUM, front_sum_part, front_sum_got)
        pair_sum(FRONT_SOLVE, front_solve_part, front_solve_pair, fill_blocks(residual, fi_stacked))
        yield
        pair_done(FRONT_SOLVE, front_solve_part, front_solve_pair)
        chip_send(FRONT_SOLVE, front_solve_part, front_solve_got)
        if stream == 0:
            loads[6].wait()
            level_part = level_rows // devs
            for level in range(2):
                split_rows(front_couple, fc_stacked.at[level], level_part, level * level_rows)
        yield
        front_forward = total(FRONT_SOLVE, front_solve_part, front_solve_got)

        pair_sum(
            RAISE_TOP, raise_top_part, raise_top_pair, fill_blocks(front_forward, fc_stacked.at[1])
        )
        yield
        pair_done(RAISE_TOP, raise_top_part, raise_top_pair)
        chip_send(RAISE_TOP, raise_top_part, raise_top_got)
        pair_sum(
            RAISE_LOW, raise_low_part, raise_low_pair, fill_blocks(front_forward, fc_stacked.at[0])
        )
        if stream == 0:
            for place in (7, 8, 9):
                loads[place].wait()
            settle(pair_recv_sem.at[stream, ROOT_SWAP], root_halves.at[:, 0])
            for matrix in range(3):
                split_root(matrix)
        yield
        pair_done(RAISE_LOW, raise_low_part, raise_low_pair)

        def less_right(level, values):
            return values - jnp.where(group == 0, root_right[own_rows, level, :], 0.0)

        yield
        raised_top = total(RAISE_TOP, raise_top_part, raise_top_got)
        share_quad(RAISE_TOP_QUAD, less_right(1, raised_top), raise_top_quad)
        chip_send(RAISE_LOW, raise_low_part, raise_low_got)

        yield
        residual = -pair_quad(RAISE_TOP_QUAD, raise_top_quad)
        send_pieces(TOP_SUM, product(residual, root_stacked[top_inverse]), top_part, top_got)
        raised_low = total(RAISE_LOW, raise_low_part, raise_low_got)
        share_quad(RAISE_LOW_QUAD, less_right(0, raised_low), raise_low_quad)
        yield
        share_pieces(TOP_SUM, TOP_SHARE, top_part, top_got, top_share)
        low_right = -pair_quad(RAISE_LOW_QUAD, raise_low_quad)

        yield
        top_forward = shared_pieces(TOP_SHARE, top_share)
        share_quad(PUSH_QUAD, product_transposed(top_forward, root_stacked[couple]), push_quad)
        yield
        residual = low_right - total_quad(PUSH_QUAD, push_quad)
        send_pieces(LOW_SUM, product(residual, root_stacked[low_inverse]), low_part, low_got)
        yield
        share_pieces(LOW_SUM, LOW_SHARE, low_part, low_got, low_share)

        yield
        low_forward = shared_pieces(LOW_SHARE, low_share)
        back = product_transposed(low_forward, root_stacked[low_inverse])
        share_quad(LOW_BACK_QUAD, back, low_back_quad)
        yield
        low_pair = total_quad(LOW_BACK_QUAD, low_back_quad)
        send_pieces(CORRECT_SUM, product(low_pair, root_stacked[couple]), correct_part, correct_got)
        low_solution = own_side(low_pair)
        root_out[own_rows, 0, :] = low_solution
        yield
        share_pieces(CORRECT_SUM, CORRECT_SHARE, correct_part, correct_got, correct_share)
        share(LOW_ALL, low_solution, low_all)
        yield
        residual = whole_pieces(top_share) - shared_pieces(CORRECT_SHARE, correct_share)
        back = product_transposed(residual, root_stacked[top_inverse])
        share_quad(TOP_BACK_QUAD, back, top_back_quad)
        share_pair(LOW_ALL, low_all)
        yield
        top_solution = own_side(total_quad(TOP_BACK_QUAD, top_back_quad))
        share(TOP_ALL, top_solution, top_all)
        root_out[own_rows, 1, :] = top_solution
        lifted = half_product(low_all, fc_stacked.at[0], core)
        pair_arrived(LOW_ALL, low_all)
        lifted = lifted + half_product(low_all, fc_stacked.at[0], other)

        lifted = lifted + (yield from gathered_product(TOP_ALL, top_all, fc_stacked.at[1]))
        share(REMAINDER_ALL, front_forward - lifted, remainder_all)
        front_values = yield from gathered_product(REMAINDER_ALL, remainder_all, fi_stacked)
        share(FRONT_ALL, front_values, front_all)
        yield
        share_pair(FRONT_ALL, front_all)
        yield
        pair_arrived(FRONT_ALL, front_all)
        for owner in range(devs):
            front_out[own_rows, owner * front_part : (owner + 1) * front_part] = front_all[
                owner % 2, owner // 2
            ]

        solutions = [None] * blocks_here
        for k in reversed(range(blocks_here)):
            picked = jnp.zeros((columns, width), F32)
            for block in range(blocks_front):
                picked = picked + jnp.where(
                    targets[k] == block, front_out[own_rows, block * width : (block + 1) * width], 0.0
                )
            residual = solved[k] - product_transposed(picked, stack(leaf_front[k]))
            if k < blocks_here - 1:
                above = jnp.zeros((columns, width), F32)
                for upper in range(k + 1, blocks_here):
                    above = above + jnp.where(parents[k] == upper, solutions[upper], 0.0)
                residual = residual - product_transposed(above, stack(leaf_link[k]))
            solutions[k] = jnp.where(k < live, product_transposed(residual, stack(leaf_inverse[k])), 0.0)
            leaf_out[own_rows, k * width : (k + 1) * width] = solutions[k]

        yield
        for phase, buffer in (
            (FRONT_SUM, front_sum_part),
            (FRONT_SOLVE, front_solve_part),
            (RAISE_TOP, raise_top_part),
            (RAISE_LOW, raise_low_part),
            (LOW_ALL, low_all),
            (TOP_ALL, top_all),
            (REMAINDER_ALL, remainder_all),
            (FRONT_ALL, front_all),
        ):
            settle(send_sem.at[stream, phase], buffer.at[0, pl.ds(1, chips - 1)])
            settle(pair_send_sem.at[stream, phase], buffer.at[0])
        for phase, buffer in (
            (TOP_SUM, top_part),
            (TOP_SHARE, top_share),
            (LOW_SUM, low_part),
            (LOW_SHARE, low_share),
            (CORRECT_SUM, correct_part),
            (CORRECT_SHARE, correct_share),
        ):
            settle(send_sem.at[stream, phase], buffer.at[pl.ds(1, chips - 1)])
        for phase, buffer in (
            (RAISE_TOP_QUAD, raise_top_quad),
            (RAISE_LOW_QUAD, raise_low_quad),
            (PUSH_QUAD, push_quad),
            (LOW_BACK_QUAD, low_back_quad),
            (TOP_BACK_QUAD, top_back_quad),
        ):
            settle(send_sem.at[stream, phase], buffer.at[pl.ds(1, quads - 1)])
        if stream == 0:
            settle(pair_send_sem.at[stream, ROOT_SWAP], root_halves.at[:, 0])

    waiting = [solve(stream) for stream in range(STREAMS)]
    while waiting:
        waiting = [steps for steps in waiting if next(steps, True) is None]


def body(
    groups,
    devs,
    leaf_right,
    leaf_inverse,
    leaf_link,
    leaf_front,
    parents,
    front_rows,
    live_blocks,
    front_right,
    front_inverse,
    front_couple,
    root_right,
    root_inverse,
    root_couple,
):
    columns = leaf_right.shape[0]
    front_part = front_right.shape[1]
    level_part = root_right.shape[2]
    level_columns = root_inverse.shape[2]
    row_tiles = columns // STREAMS // ROW_TILE
    piece = level_columns // 2 * row_tiles // (devs // 2)
    own = columns // STREAMS
    loaded = (
        leaf_right,
        leaf_inverse,
        leaf_link,
        leaf_front,
        front_right,
        front_inverse,
        front_couple,
        root_inverse,
        root_couple,
    )
    rows, half = front_inverse.shape[0], front_inverse.shape[1] // 2
    level_half = front_couple.shape[1] // 4
    root_rows, root_half = root_inverse.shape[1], level_columns // 2
    halves = (
        (2, 2 * rows, half),
        (2, 2, 2 * rows, level_half),
        (3, 4 * root_rows, root_half),
    )
    chips = devs // 2
    front_full = pltpu.VMEM((STREAMS, 2, chips, own, front_part), F32)
    front_half = pltpu.VMEM((STREAMS, chips, own, front_part), F32)
    level_full = pltpu.VMEM((STREAMS, 2, chips, own, level_part), F32)
    level_half_blocks = pltpu.VMEM((STREAMS, chips, own, level_part), F32)
    pieces_half = pltpu.VMEM((STREAMS, chips, ROW_TILE, piece), F32)
    quad_blocks = pltpu.VMEM((STREAMS, 2 * groups, own, level_part), F32)
    quad_pairs = pltpu.VMEM((STREAMS, 2 * groups, own, 2 * level_part), F32)
    vmem = pl.BlockSpec(memory_space=pltpu.VMEM)
    smem = pl.BlockSpec(memory_space=pltpu.SMEM)
    anywhere = pl.BlockSpec(memory_space=pltpu.HBM)
    results = (
        jax.ShapeDtypeStruct(leaf_right.shape, F32),
        jax.ShapeDtypeStruct((columns, front_part * devs), F32),
        jax.ShapeDtypeStruct(root_right.shape, F32),
    )
    return pl.pallas_call(
        functools.partial(kernel, groups, devs),
        out_shape=results,
        in_specs=[smem] * 3 + [vmem] + [anywhere] * len(loaded),
        out_specs=(vmem, vmem, vmem),
        scratch_shapes=[pltpu.VMEM(array.shape, F32) for array in loaded[:-2]]
        + [pltpu.VMEM((3, 2, root_rows, root_half), F32)]
        + [pltpu.VMEM(shape, BF16) for shape in halves]
        + [pltpu.VMEM((STREAMS, leaf_inverse.shape[0], own, leaf_inverse.shape[1]), F32)]
        + [front_full] * 2
        + [front_half] * 4
        + [level_full] * 2
        + [level_half_blocks] * 4
        + [pieces_half] * 9
        + [quad_blocks] * 2
        + [quad_pairs] * 3
        + [level_full] * 2
        + [front_full] * 2
        + [
            pltpu.SemaphoreType.DMA((len(loaded) + 1,)),
        ]
        + [pltpu.SemaphoreType.DMA((STREAMS, PHASES))] * 4,
        compiler_params=pltpu.CompilerParams(
            collective_id=0, has_side_effects=True, vmem_limit_bytes=60 * 1024 * 1024
        ),
        name="block_solves",
    )(parents, front_rows, live_blocks, root_right, *loaded)


def solution(mesh):
    in_specs = (
        P(None, ("grp", "dev")),
        P(("grp", "dev"), None, None),
        P(("grp", "dev"), None, None),
        P(("grp", "dev"), None, None),
        P(("grp", "dev")),
        P(("grp", "dev")),
        P(("grp", "dev")),
        P(None, ("grp", "dev")),
        P(("grp", "dev"), None),
        P(("grp", "dev"), None),
        P(None, None, "dev"),
        P(None, "dev", "grp"),
        P(None, "dev", "grp"),
    )
    out_specs = (P(None, ("grp", "dev")), P(None, "grp"), P(None, None, "dev"))
    return jax.shard_map(
        functools.partial(body, mesh.shape["grp"], mesh.shape["dev"]),
        mesh=mesh,
        in_specs=in_specs,
        out_specs=out_specs,
        check_vma=False,
    )
```

time: 590 us -> 88.3 us (0.15)
  waiting for transfers between devices: 434 us -> 0 us
  blocking collectives: 88.6 us -> 0 us
  Pallas kernels: 0 us -> 82.2 us
  matrix products: 25.4 us -> 0 us
  loops' own time: 14.7 us -> 0 us
  between operations: 15 us -> 1.29 us
  local copies, waits for them, and re-layouts: 10.4 us -> 4.42 us
    psum x3 -> x0, waiting for transfers between devices: 267 us -> none  [the longest x2 179 us: body(): lax.psum(jnp.dot(residual, root_inverse[height], precision=EXACT_ARITHMET...]
    reduce_scatter x3 -> x0, waiting for transfers between devices: 167 us -> none  [the longest x1 56.3 us: body(): lax.psum_scatter(front_terms, 'dev', scatter_dimension=1, tiled=True)]
    pallas_call x0 -> x1, Pallas kernels: none -> 82.2 us  [body(): pl.pallas_call(functools.partial(kernel, groups, devs), out_shape=results...]
    all_gather x3 -> x0, blocking collectives: 63.3 us -> none  [the longest x1 25.5 us: body(): lax.all_gather(root_solution, 'dev', axis=2, tiled=True)]
    dot_general x22 -> x0, matrix products: 25.4 us -> none  [the longest x2 4.19 us: body(): jnp.dot(residual, root_inverse[height], precision=EXACT_ARITHMETIC)]
    psum x4 -> x0, blocking collectives: 25.3 us -> none  [the longest x2 12.2 us: body(): lax.psum(jnp.einsum('rj,ij->ri', residual, root_inverse[height], precisio...]
    another operation x2 -> x0, loops' own time: 14.7 us -> none  [the longest x1 7.4 us: piece_forward(): return lax.fori_loop(0, upper_bound, advance, (empty_state, empty_state))[1]]
  transfers between devices with their start and end apart: 6 -> 0, of which waited for: 6 -> 0; matrix products, arithmetic and copies ran while one was open for 0% -> 0% of each run, Pallas kernels for 0% -> 0%
where the time goes in v4:
time: 88.3 us; the launch traced here: 88 us
  Pallas kernels  82.2 us (93%)
  local copies, waits for them, and re-layouts  4.42 us (5%)
  between operations  1.29 us (1%)
    pallas_call x1, Pallas kernels, body(): pl.pallas_call(functools.partial(kernel, groups, devs), out_shape=results...  82.2 us
    unnamed x3, local copies, waits for them, and re-layouts  4.42 us

profile of v4, /device:TPU:1, one launch (start us, length us, event | category | flops | bytes accessed | tf_op | source)
XLA Modules:
  0.0 88.0 jit_solution(7862829258519771388)
XLA Ops:
  1.3 82.2 %block_solves.1 = (f32[32,256]{1,0:T(8,128)}, f32[32,2048]{1,0:T(8,128)}, f32[32,2,128]{2,1,0:T(2,128)}) custom-call(s32[2]{0:T(128)} %parents.1, s32[2]{0:T(128)} %targets.1, s32[1]{0:T(128)S(6)} %copy.19.live_blocks, f32[32,2,128]{2,1,0:T(2,128)} %root_right.1, f32[32,256]{1,0:T(8,128)} %leaf_right_hbm.1, f32[2,128,128]{2,1,0:T(8,128)} %leaf_inverse_hbm.1, ...), custom_call_target="tpu_custom_call" | custom-call | tf_op jit(solution)/shard_map/block_solves/pallas_call | solution.py:627
  83.5 1.4 %copy.20 = f32[32,256]{1,0:T(8,128)} copy(f32[32,256]{1,0:T(8,128)} %get-tuple-element.6) | data formatting | bytes 65536
  84.9 1.7 %copy.21 = f32[32,2048]{1,0:T(8,128)} copy(f32[32,2048]{1,0:T(8,128)} %get-tuple-element.7) | data formatting | bytes 524288
  86.6 1.4 %copy.22 = f32[32,2,128]{2,1,0:T(2,128)} copy(f32[32,2,128]{2,1,0:T(2,128)} %get-tuple-element.8) | data formatting | bytes 65536

commit v5 on v4

--- a/solution.py
+++ b/solution.py
@@ -63,6 +63,13 @@
     )
     result = result[:rows] + result[rows:]
     return result[:, :depth] + result[:, depth:]
+
+
+def product_turned(left, turned):
+    rows, width = left.shape[0], turned.shape[1] // 2
+    result = jnp.dot(jnp.concatenate(split(left), 0), turned, preferred_element_type=F32)
+    result = result[:rows] + result[rows:]
+    return result[:, :width] + result[:, width:]
 
 
 def stack(values):
@@ -99,6 +106,9 @@
     fi_stacked,
     fc_stacked,
     root_stacked,
+    fi_turned,
+    fc_turned,
+    root_turned,
     *rest,
 ):
     *buffers, load_sem, send_sem, recv_sem, pair_send_sem, pair_recv_sem = rest
@@ -321,6 +331,12 @@
 
             lax.fori_loop(0, count // step_rows, one, 0)
 
+        def turn(source, target):
+            step = min(source.shape[1], 256)
+            for at in range(0, source.shape[1], step):
+                here = source[:, at : at + step].astype(F32)
+                target[at : at + step, :] = here.T.astype(BF16)
+
         def fill_blocks(left, stacked):
             def fill(side, part):
                 count, span = part.shape[0], part.shape[2]
@@ -365,7 +381,7 @@
             return whole_pieces(buffer)
 
         def half_product(buffer, stacked, side):
-            return product_transposed(whole(buffer, side), stacked[side])
+            return product_turned(whole(buffer, side), stacked[side])
 
         def gathered_product(phase, buffer, stacked):
             yield
@@ -444,6 +460,7 @@
             settle(pair_recv_sem.at[stream, ROOT_SWAP], root_halves.at[:, 0])
             for matrix in range(3):
                 split_root(matrix)
+            turn(root_stacked.at[couple], root_turned.at[couple])
         yield
         pair_done(RAISE_LOW, raise_low_part, raise_low_pair)
 
@@ -458,6 +475,9 @@
         yield
         residual = -pair_quad(RAISE_TOP_QUAD, raise_top_quad)
         send_pieces(TOP_SUM, product(residual, root_stacked[top_inverse]), top_part, top_got)
+        if stream == 0:
+            turn(root_stacked.at[low_inverse], root_turned.at[low_inverse])
+            turn(root_stacked.at[top_inverse], root_turned.at[top_inverse])
         raised_low = total(RAISE_LOW, raise_low_part, raise_low_got)
         share_quad(RAISE_LOW_QUAD, less_right(0, raised_low), raise_low_quad)
         yield
@@ -466,20 +486,29 @@
 
         yield
         top_forward = shared_pieces(TOP_SHARE, top_share)
-        share_quad(PUSH_QUAD, product_transposed(top_forward, root_stacked[couple]), push_quad)
+        share_quad(PUSH_QUAD, product_turned(top_forward, root_turned[couple]), push_quad)
         yield
         residual = low_right - total_quad(PUSH_QUAD, push_quad)
         send_pieces(LOW_SUM, product(residual, root_stacked[low_inverse]), low_part, low_got)
+        if stream == 0:
+            for side in range(2):
+                turn(fc_stacked.at[0, side], fc_turned.at[0, side])
         yield
         share_pieces(LOW_SUM, LOW_SHARE, low_part, low_got, low_share)
+        if stream == 0:
+            for side in range(2):
+                turn(fc_stacked.at[1, side], fc_turned.at[1, side])
 
         yield
         low_forward = shared_pieces(LOW_SHARE, low_share)
-        back = product_transposed(low_forward, root_stacked[low_inverse])
+        back = product_turned(low_forward, root_turned[low_inverse])
         share_quad(LOW_BACK_QUAD, back, low_back_quad)
         yield
         low_pair = total_quad(LOW_BACK_QUAD, low_back_quad)
         send_pieces(CORRECT_SUM, product(low_pair, root_stacked[couple]), correct_part, correct_got)
+        if stream == 0:
+            for side in range(2):
+                turn(fi_stacked.at[side], fi_turned.at[side])
         low_solution = own_side(low_pair)
         root_out[own_rows, 0, :] = low_solution
         yield
@@ -487,20 +516,20 @@
         share(LOW_ALL, low_solution, low_all)
         yield
         residual = whole_pieces(top_share) - shared_pieces(CORRECT_SHARE, correct_share)
-        back = product_transposed(residual, root_stacked[top_inverse])
+        back = product_turned(residual, root_turned[top_inverse])
         share_quad(TOP_BACK_QUAD, back, top_back_quad)
         share_pair(LOW_ALL, low_all)
         yield
         top_solution = own_side(total_quad(TOP_BACK_QUAD, top_back_quad))
         share(TOP_ALL, top_solution, top_all)
         root_out[own_rows, 1, :] = top_solution
-        lifted = half_product(low_all, fc_stacked.at[0], core)
+        lifted = half_product(low_all, fc_turned.at[0], core)
         pair_arrived(LOW_ALL, low_all)
-        lifted = lifted + half_product(low_all, fc_stacked.at[0], other)
-
-        lifted = lifted + (yield from gathered_product(TOP_ALL, top_all, fc_stacked.at[1]))
+        lifted = lifted + half_product(low_all, fc_turned.at[0], other)
+
+        lifted = lifted + (yield from gathered_product(TOP_ALL, top_all, fc_turned.at[1]))
         share(REMAINDER_ALL, front_forward - lifted, remainder_all)
-        front_values = yield from gathered_product(REMAINDER_ALL, remainder_all, fi_stacked)
+        front_values = yield from gathered_product(REMAINDER_ALL, remainder_all, fi_turned)
         share(FRONT_ALL, front_values, front_all)
         yield
         share_pair(FRONT_ALL, front_all)
@@ -632,6 +661,7 @@
         scratch_shapes=[pltpu.VMEM(array.shape, F32) for array in loaded[:-2]]
         + [pltpu.VMEM((3, 2, root_rows, root_half), F32)]
         + [pltpu.VMEM(shape, BF16) for shape in halves]
+        + [pltpu.VMEM(shape[:-2] + (shape[-1], shape[-2]), BF16) for shape in halves]
         + [pltpu.VMEM((STREAMS, leaf_inverse.shape[0], own, leaf_inverse.shape[1]), F32)]
         + [front_full] * 2
         + [front_half] * 4

time: 88.3 us -> 87.3 us (0.989)
  Pallas kernels: 82.2 us -> 81.2 us
    pallas_call x1, Pallas kernels: 82.2 us -> 81.2 us  [body(): pl.pallas_call(functools.partial(kernel, groups, devs), out_shape=results...]
where the time goes in v5:
time: 87.3 us; the launch traced here: 86.9 us
  Pallas kernels  81.2 us (93%)
  local copies, waits for them, and re-layouts  4.42 us (5%)
  between operations  1.29 us (1%)
    pallas_call x1, Pallas kernels, body(): pl.pallas_call(functools.partial(kernel, groups, devs), out_shape=results...  81.2 us
    unnamed x3, local copies, waits for them, and re-layouts  4.42 us

profile of v5, /device:TPU:1, one launch (start us, length us, event | category | flops | bytes accessed | tf_op | source)
XLA Modules:
  0.0 86.9 jit_solution(6857927029544911868)
XLA Ops:
  1.3 81.2 %block_solves.1 = (f32[32,256]{1,0:T(8,128)}, f32[32,2048]{1,0:T(8,128)}, f32[32,2,128]{2,1,0:T(2,128)}) custom-call(s32[2]{0:T(128)} %parents.1, s32[2]{0:T(128)} %targets.1, s32[1]{0:T(128)S(6)} %copy.19.live_blocks, f32[32,2,128]{2,1,0:T(2,128)} %root_right.1, f32[32,256]{1,0:T(8,128)} %leaf_right_hbm.1, f32[2,128,128]{2,1,0:T(8,128)} %leaf_inverse_hbm.1, ...), custom_call_target="tpu_custom_call" | custom-call | tf_op jit(solution)/shard_map/block_solves/pallas_call | solution.py:656
  82.5 1.4 %copy.20 = f32[32,256]{1,0:T(8,128)} copy(f32[32,256]{1,0:T(8,128)} %get-tuple-element.6) | data formatting | bytes 65536
  83.9 1.7 %copy.21 = f32[32,2048]{1,0:T(8,128)} copy(f32[32,2048]{1,0:T(8,128)} %get-tuple-element.7) | data formatting | bytes 524288
  85.6 1.4 %copy.22 = f32[32,2,128]{2,1,0:T(2,128)} copy(f32[32,2,128]{2,1,0:T(2,128)} %get-tuple-element.8) | data formatting | bytes 65536
